TPU v7x, 1024 devices: a whole 8x8x8 slice. The times are simulated.
1024 devices in a mesh: expert: 64 (over z, x), dp: 16 (over y, core).
Axes of the slice: x: 8, y: 8, z: 8, core: 2. Of those that a mesh axis runs over, the one named last changes fastest.
Arguments:
- expert_hidden: bfloat16 [192, 768, 1024], P('expert'), may hold values from -6 to 6
- down_weight: bfloat16 [128, 1024, 3584], P('expert', None, 'dp'), may hold values from -0.1875 to 0.1875
- out_grad: bfloat16 [6144, 3584], P('expert', 'dp'), may hold values from -6 to 6
- expert_ids: int32 [6144, 8], P('expert'), may hold values from 0 to 127, all different within a row; in each aligned block of 96 rows (0 to 95, 96 to 191, ...) at most 12 rows name the same one
- gate_code: int32 [6144, 8], P('expert'), may hold values from 0 to 15
- expert_load: int32 [128], replicated, may hold values from 0 to 999999
Outputs:
- mixed: bfloat16 [6144, 3584], P('expert', 'dp')
- hidden_grad: bfloat16 [192, 768, 1024], P('expert', 'dp')
- weight_grad: bfloat16 [128, 1024, 3584], P('expert', None, 'dp')
- spare_grad: bfloat16 [64, 1024, 3584], P('expert', None, 'dp')
Inputs may be any that keep to these rules, and one draw needn't show every extreme that they name: `expert_ids`: each token's 8 picks are different experts; among the picks of the 96 tokens of one index of expert no expert appears more than 12 times, and in some such block an expert appears exactly 12 times.
All inputs are finite; a program needn't handle non-finite values.
Results may differ from a plain program's by a relative error of at most 0.022.
Values may be sent and summed in bfloat16 or wider, within the bound.
A program may use at most 64 MiB of HBM per device.

v0:
```python
import jax
import jax.numpy as jnp
from jax import lax
from jax.sharding import PartitionSpec as P


def partner(array, axis, apart):
    return lax.ppermute(array, axis, [(i, i ^ 1 << apart) for i in range(lax.axis_size(axis))])


def body(expert_hidden, down_weight, out_grad, expert_ids, gate_code, expert_load):
    members = lax.axis_size("expert")
    halfway = members // 2
    device = lax.axis_index("expert")
    local_count = down_weight.shape[0]
    slot_count = local_count + 1
    tok_rows, picks = expert_ids.shape
    capacity = expert_hidden.shape[1] // members
    columns = out_grad.shape[1]
    hottest = jnp.argmax(expert_load.reshape(members, local_count), axis=1)
    device_ids = jnp.arange(members, dtype=jnp.int32)
    home_dev = expert_ids // local_count
    home_slot = expert_ids % local_count
    hot_home = jnp.sum(jnp.where(home_dev[:, :, None] == device_ids, hottest, 0), axis=-1)
    spare_use = (home_slot == hot_home) & (device // halfway != home_dev // halfway)
    target = jnp.where(spare_use, jnp.bitwise_xor(home_dev, halfway), home_dev).reshape(-1)
    dest_slot = jnp.where(spare_use, local_count, home_slot).reshape(-1)
    slot_ids = dest_slot * members + target
    labels = jnp.arange(slot_count * members, dtype=jnp.int32)
    one_hot = (slot_ids[:, None] == labels[None, :]).astype(jnp.int32)
    place = jnp.sum((jnp.cumsum(one_hot, axis=0) - one_hot) * one_hot, axis=1)
    gate_value = 0.0625 * (gate_code.astype(jnp.float32) + 1.0)
    grad_rows = (gate_value[:, :, None] * out_grad[:, None, :].astype(jnp.float32)).astype(
        jnp.bfloat16
    )
    grad_rows = grad_rows.reshape(tok_rows * picks, columns)
    outgoing = jnp.zeros((slot_count, members, capacity, columns), jnp.bfloat16)
    outgoing = outgoing.at[dest_slot, target, place].set(grad_rows)
    arrived = lax.all_to_all(outgoing, "expert", split_axis=1, concat_axis=1, tiled=True)
    arrived = arrived.reshape(slot_count, members * capacity, columns)
    my_hot = lax.dynamic_index_in_dim(hottest, device, 0, keepdims=False)
    hot_weight = lax.dynamic_index_in_dim(down_weight, my_hot, 0, keepdims=False)
    copy_weight = partner(hot_weight, "expert", members.bit_length() - 2)
    slot_weights = jnp.concatenate([down_weight, copy_weight[None]], axis=0)
    outputs = jnp.einsum(
        "srh,shd->srd", expert_hidden, slot_weights, preferred_element_type=jnp.float32
    ).astype(jnp.bfloat16)
    returned = lax.all_to_all(
        outputs.reshape(slot_count, members, capacity, columns),
        "expert",
        split_axis=1,
        concat_axis=1,
        tiled=True,
    )
    gathered = returned[dest_slot, target, place].reshape(tok_rows, picks, columns)
    mixed_sum = jnp.sum(gate_value[:, :, None] * gathered.astype(jnp.float32), axis=1).astype(
        jnp.bfloat16
    )
    partial_value = jnp.einsum(
        "srd,shd->srh", arrived, slot_weights, preferred_element_type=jnp.float32
    )
    hidden_sums = lax.psum_scatter(
        partial_value.astype(jnp.bfloat16), "dp", scatter_dimension=1, tiled=True
    )
    grad_scale = local_count / tok_rows
    slot_grad = (
        grad_scale
        * jnp.einsum("srh,srd->shd", expert_hidden, arrived, preferred_element_type=jnp.float32)
    ).astype(jnp.bfloat16)
    weight_grad = slot_grad[:local_count]
    spare_grad = slot_grad[local_count:]
    return (mixed_sum, hidden_sums, weight_grad, spare_grad)


def solution(mesh):
    placed = (
        P("expert", None, None),
        P("expert", None, "dp"),
        P("expert", "dp"),
        P("expert", None),
        P("expert", None),
        P(),
    )
    return jax.shard_map(
        body,
        mesh=mesh,
        in_specs=placed,
        out_specs=(
            P("expert", "dp"),
            P("expert", "dp", None),
            P("expert", None, "dp"),
            P("expert", None, "dp"),
        ),
        check_vma=False,
    )
```

profile of v0, /device:TPU:14, one launch (start us, length us, event | category | flops | bytes accessed | tf_op | source)
XLA Modules:
  0.0 224.7 jit_solution(6165971556724176875)
XLA Ops:
  7.2 0.8 reshape.136
  8.6 0.7 add_select_fusion.1
  9.4 0.7 multiply_add_fusion
  12.5 48.2 %scatter_fusion = bf16[3,64,12,224]{3,1,2,0:T(8,128)(2,1)S(1)} fusion(bf16[3,64,12,224]{3,1,2,0:T(8,128)(2,1)S(1)} %broadcast_in_dim.17, s32[768]{0:T(1024)S(1)} %get-tuple-element.6, bf16[768,224]{1,0:T(8,128)(2,1)S(1)} %fusion.5), kind=kCustom, calls=%fused_computation.1 | custom fusion | bytes 1041408 | tf_op jit(solution)/shard_map/scatter | solution.py:38
  60.7 1.8 copy.55
  62.6 22.6 %all-to-all-start.1 = ((bf16[3,64,12,224]{3,2,0,1:T(8,128)(2,1)}), bf16[3,64,12,224]{3,2,0,1:T(8,128)(2,1)S(1)}, u32[]{:S(2)}, u32[]{:S(2)}) async-start(bf16[3,64,12,224]{3,2,0,1:T(8,128)(2,1)} %copy.55), calls=%async_computation.1 | async-start | bytes 3145728 | tf_op jit(solution)/shard_map/all_to_all | solution.py:39
  87.8 0.8 dynamic-slice_bitcast_fusion
  88.6 7.4 %collective-permute-start = (bf16[1024,224]{0,1:T(8,128)(2,1)}, bf16[1024,224]{0,1:T(8,128)(2,1)}, u32[]{:S(2)}, u32[]{:S(2)}) collective-permute-start(bf16[1024,224]{0,1:T(8,128)(2,1)} %dynamic-slice_bitcast_fusion), channel_id=1, source_target_pairs={{0,512},{16,528},{32,544},{48,560},{64,576},{80,592},{96,608},{112... | collective-permute-start | bytes 1376264 | tf_op jit(solution)/shard_map/ppermute | solution.py:8
  96.1 30.6 %all-to-all-done.1 = bf16[3,64,12,224]{3,2,0,1:T(8,128)(2,1)S(1)} async-done(((bf16[3,64,12,224]{3,2,0,1:T(8,128)(2,1)}), bf16[3,64,12,224]{3,2,0,1:T(8,128)(2,1)S(1)}, u32[]{:S(2)}, u32[]{:S(2)}) %all-to-all-start.1) | async-done | bytes 1032224 | tf_op jit(solution)/shard_map/all_to_all | solution.py:39
  127.5 16.4 %collective-permute-done = bf16[1024,224]{0,1:T(8,128)(2,1)} collective-permute-done((bf16[1024,224]{0,1:T(8,128)(2,1)}, bf16[1024,224]{0,1:T(8,128)(2,1)}, u32[]{:S(2)}, u32[]{:S(2)}) %collective-permute-start) | collective-permute-done | bytes 458784 | tf_op jit(solution)/shard_map/ppermute | solution.py:8
  143.9 4.8 %convolution_convert_fusion = bf16[3,768,1024]{2,1,0:T(8,128)(2,1)} fusion(bf16[3,768,224]{2,1,0:T(8,128)(2,1)S(1)} %reshape.141, bf16[1,1024,224]{1,2,0:T(8,128)(2,1)} %bitcast.2, bf16[2,1024,224]{1,2,0:T(8,128)(2,1)} %param.7), kind=kOutput, calls=%fused_computation.2 | convolution fusion | flops 1060012032 | bytes 7127040 | tf_op jit(solution)/shard_map/srd,shd->srh/dot_general | solution.py:59
  148.8 1.2 copy-done.1
  149.9 4.1 %fusion.1 = bf16[3,768,224]{1,2,0:T(8,128)(2,1)S(1)} fusion(bf16[3,768,1024]{2,1,0:T(8,128)(2,1)} %param.6, bf16[1,1024,224]{1,2,0:T(8,128)(2,1)} %bitcast.2, bf16[2,1024,224]{1,2,0:T(8,128)(2,1)S(1)} %copy-done.1), kind=kOutput, calls=%fused_computation.7 | convolution fusion | flops 1058168832 | bytes 7127040 | tf_op jit(solution)/shard_map/srh,shd->srd/dot_general | solution.py:45
  154.0 1.4 copy.45
  155.4 2.4 %reshape.137 = bf16[3,64,12,224]{3,2,1,0:T(8,128)(2,1)S(1)} reshape(bf16[3,768,224]{2,1,0:T(8,128)(2,1)} %copy.45) | data formatting | bytes 2064384 | tf_op jit(solution)/shard_map/reshape | solution.py:49
  157.8 1.3 copy.46
  159.1 10.5 %all-to-all-start = ((bf16[3,64,12,224]{3,2,0,1:T(8,128)(2,1)}), bf16[3,64,12,224]{3,2,0,1:T(8,128)(2,1)S(1)}, u32[]{:S(2)}, u32[]{:S(2)}) async-start(bf16[3,64,12,224]{3,2,0,1:T(8,128)(2,1)} %copy.46), calls=%async_computation | async-start | bytes 3145728 | tf_op jit(solution)/shard_map/all_to_all | solution.py:48
  169.6 3.7 %fusion = bf16[3,1024,224]{1,2,0:T(8,128)(2,1)S(1)} fusion(bf16[3,768,224]{2,1,0:T(8,128)(2,1)S(1)} %reshape.141, bf16[3,768,1024]{2,1,0:T(8,128)(2,1)} %param.6), kind=kOutput, calls=%fused_computation.5 | convolution fusion | flops 1058340864 | bytes 7127040 | tf_op jit(solution)/shard_map/srh,srd->shd/dot_general | solution.py:68
  173.4 1.0 slice.24
  174.4 0.8 slice.25
  175.2 33.8 %all-to-all-done = bf16[3,64,12,224]{3,2,0,1:T(8,128)(2,1)S(1)} async-done(((bf16[3,64,12,224]{3,2,0,1:T(8,128)(2,1)}), bf16[3,64,12,224]{3,2,0,1:T(8,128)(2,1)S(1)}, u32[]{:S(2)}, u32[]{:S(2)}) %all-to-all-start) | async-done | bytes 1032224 | tf_op jit(solution)/shard_map/all_to_all | solution.py:48
  209.4 5.2 %gather_fusion = bf16[768,224]{1,0:T(8,128)(2,1)S(1)} fusion(bf16[3,64,12,224]{3,1,2,0:T(8,128)(2,1)S(1)} %copy.53, s32[768]{0:T(1024)S(1)} %get-tuple-element.7), kind=kCustom, calls=%fused_computation | custom fusion | bytes 697344 | tf_op jit(solution)/shard_map/gather | solution.py:55
  214.6 1.0 fusion.4
  215.6 2.2 reduce-scatter.2.cloned.1.call-done
  (36 shorter events, 4.9 us)
Async XLA Ops:
  10.8 1.0 copy-start.3
  10.8 1.1 copy-start.2
  62.6 25.2 %copy-start = (bf16[2,1024,224]{1,2,0:T(8,128)(2,1)S(1)}, bf16[2,1024,224]{1,2,0:T(8,128)(2,1)}, u32[]{:S(2)}) copy-start(bf16[2,1024,224]{1,2,0:T(8,128)(2,1)} %param.7) | copy-start | bytes 2752516
  62.6 64.1 %all-to-all-start.1 = ((bf16[3,64,12,224]{3,2,0,1:T(8,128)(2,1)}), bf16[3,64,12,224]{3,2,0,1:T(8,128)(2,1)S(1)}, u32[]{:S(2)}, u32[]{:S(2)}) async-start(bf16[3,64,12,224]{3,2,0,1:T(8,128)(2,1)} %copy.55), calls=%async_computation.1 | async-start | bytes 3145728 | tf_op jit(solution)/shard_map/all_to_all | solution.py:39
  85.2 132.6 %reduce-scatter.2.cloned.1.call-start = ((), (), s32[]{:S(2)}) async-start(), calls=%async_computation.3 | async-start | bytes 5013504 | tf_op jit(solution)/shard_map/reduce_scatter | solution.py:62
  88.6 55.2 %collective-permute-start = (bf16[1024,224]{0,1:T(8,128)(2,1)}, bf16[1024,224]{0,1:T(8,128)(2,1)}, u32[]{:S(2)}, u32[]{:S(2)}) collective-permute-start(bf16[1024,224]{0,1:T(8,128)(2,1)} %dynamic-slice_bitcast_fusion), channel_id=1, source_target_pairs={{0,512},{16,528},{32,544},{48,560},{64,576},{80,592},{96,608},{112... | collective-permute-start | bytes 1376264 | tf_op jit(solution)/shard_map/ppermute | solution.py:8
  148.7 1.2 copy-start.1
  159.1 49.9 %all-to-all-start = ((bf16[3,64,12,224]{3,2,0,1:T(8,128)(2,1)}), bf16[3,64,12,224]{3,2,0,1:T(8,128)(2,1)S(1)}, u32[]{:S(2)}, u32[]{:S(2)}) async-start(bf16[3,64,12,224]{3,2,0,1:T(8,128)(2,1)} %copy.46), calls=%async_computation | async-start | bytes 3145728 | tf_op jit(solution)/shard_map/all_to_all | solution.py:48
Sparse Core Ops, SparseCore 0:
  148.9 68.9 reduce-scatter.1
where the time goes:
time: 226 us; the launch traced here: 225 us
  waiting for transfers between devices  83.1 us (37%)
  local copies, waits for them, and re-layouts  68.3 us (30%)
  starting transfers between devices  40.6 us (18%)
  between operations  16.2 us (7%)
  matrix products  12.7 us (6%)
  other arithmetic  3.8 us (2%)
    scatter x2, local copies, waits for them, and re-layouts, body(): outgoing = outgoing.at[dest_slot, target, place].set(grad_rows)  50 us
    all_to_all x1, waiting for transfers between devices, body(): lax.all_to_all(outputs.reshape(slot_count, members, capacity, columns), '...  33.8 us
    all_to_all x1, waiting for transfers between devices, body(): lax.all_to_all(outgoing, 'expert', split_axis=1, concat_axis=1, tiled=True)  30.6 us
    all_to_all x1, starting transfers between devices, body(): lax.all_to_all(outgoing, 'expert', split_axis=1, concat_axis=1, tiled=True)  22.6 us
    ppermute x1, waiting for transfers between devices, partner(): lax.ppermute(array, axis, [(i, i ^ 1 << apart) for i in range(lax.axis_si...  16.4 us
    all_to_all x1, starting transfers between devices, body(): lax.all_to_all(outputs.reshape(slot_count, members, capacity, columns), '...  10.5 us
    ppermute x1, starting transfers between devices, partner(): lax.ppermute(array, axis, [(i, i ^ 1 << apart) for i in range(lax.axis_si...  7.41 us
    gather x1, local copies, waits for them, and re-layouts, body(): returned[dest_slot, target, place].reshape(tok_rows, picks, columns)  5.23 us
  transfers between devices with their start and end apart: 4, of which 4 were waited for; matrix products, arithmetic and copies ran while one was open for 10% of the time, Pallas kernels for 0%

commit v1 on v0

v1 whole, which is shorter than its diff:
```python
import jax
import jax.numpy as jnp
from jax import lax
from jax.experimental import pallas as pl
from jax.experimental.pallas import tpu as pltpu
from jax.sharding import PartitionSpec as P

MESH = pl.DeviceIdType.MESH
BF = jnp.bfloat16
F32 = jnp.float32

Z = 8
X = 8
Y = 8
TOK = 96
LANES = 128
TOP = 8
MOST = 12
H = 1024
COLS = 224
HALF = 384
BLOCK = 48
RING = 7
SIDE = 512


def dot(a, b):
    return jnp.dot(a, b, preferred_element_type=F32)


def dot_nt(a, b):
    return lax.dot_general(a, b, (((1,), (1,)), ((), ())), preferred_element_type=F32)


def dot_tn(a, b):
    return lax.dot_general(a, b, (((0,), (0,)), ((), ())), preferred_element_type=F32)


def kernel(
    hid_hbm, w_hbm, og_ref, ids_ref, code_ref, load_ref,
    mixed_ref, hg_ref, wg_hbm, sg_hbm,
    hid, hid_n, hid_h, hid_c, w, w_n, w_h, w_c,
    turn, meta, tok, perm, perm_h,
    key_n, key_h, key_c, gate_n, gate_h, gate_c, g_n, g_hc,
    out_n, out_h, out_c, send_n, send_hc, recv_n, recv_hc,
    sb_n, sb_h, sb_c, back_n, back_hc, rg_n, rg_hc,
    cxs_n, cxs_h, cxs_c, cxr_n, cxr_h, cxr_c, sum_n, sum_h, sum_c,
    rs_n, rs_h, rs_c, rr_n, rr_h, rr_c,
    mix_s, mix_r, val_h, val_c, wg, sg,
    load_sem, zt_s, zt_r, zm_s, zm_r, wc_s, wc_r,
    dn_s, dn_r, dh_s, dh_r, bn_s, bn_r, bh_s, bh_r, bc_s, bc_r,
    cx_s, cx_r, ring_s, ring_r, mx_s, mx_r, out_sem,
):
    e = lax.axis_index("expert")
    dp = lax.axis_index("dp")
    z, x, y, c = e // X, e % X, dp // 2, dp % 2
    h = z // 4

    def z_peer(d):
        return (((z + d) % Z) * X + x, dp)

    def x_peer(d):
        return (z * X + (x + d) % X, dp)

    def y_peer(d):
        return (e, ((y + d) % Y) * 2 + c)

    sibling = (e, y * 2 + 1 - c)

    def remote(src, dst, s, r, to):
        return pltpu.make_async_remote_copy(
            src_ref=src, dst_ref=dst, send_sem=s, recv_sem=r, device_id=to, device_id_type=MESH
        )

    loads = [
        pltpu.make_async_copy(w_hbm, w, load_sem.at[0]),
        pltpu.make_async_copy(hid_hbm.at[0], hid.at[0], load_sem.at[1]),
        pltpu.make_async_copy(hid_hbm.at[1], hid.at[1], load_sem.at[2]),
        pltpu.make_async_copy(
            hid_hbm.at[2, pl.ds(pl.multiple_of(h * HALF, HALF), HALF)], hid_c, load_sem.at[3]
        ),
    ]
    for copy in loads:
        copy.start()

    barrier = pltpu.get_barrier_semaphore()
    peers = [z_peer(d) for d in range(1, Z)] + [x_peer(d) for d in range(1, X)]
    peers += [y_peer(1), y_peer(-1), sibling]
    for peer in peers:
        pl.semaphore_signal(barrier, inc=1, device_id=peer, device_id_type=MESH)

    turn[...] = jnp.full((LANES, LANES), -1.0, F32)
    turn[0:TOK, 0:TOP] = ids_ref[...].astype(F32)
    turn[0:TOK, TOP : 2 * TOP] = code_ref[...].astype(F32)
    meta[z] = turn[...].T[0 : 2 * TOP]
    tok[z, 0:TOK] = og_ref[...]
    for i in range(Z):
        tok[i, TOK:LANES] = jnp.zeros((LANES - TOK, COLS), BF)

    pl.semaphore_wait(barrier, len(peers))

    gather = []
    for i, d in enumerate((4, 3, -3, 2, -2, 1, -1)):
        gather.append(remote(meta.at[z], meta.at[z], zm_s.at[i], zm_r.at[i], z_peer(d)))
        gather.append(
            remote(tok.at[z, pl.ds(0, TOK)], tok.at[z, pl.ds(0, TOK)], zt_s.at[i], zt_r.at[i], z_peer(d))
        )
    for copy in gather:
        copy.start()

    own = load_ref[pl.ds(e, 1), :]
    hot = jnp.where(own[:, 1:2] > own[:, 0:1], 1.0, 0.0)
    hot_b, cold_b = hot.astype(BF), (1.0 - hot).astype(BF)
    cold = 1.0 - hot

    loads[0].wait()
    w_h[...] = w[0] * cold_b + w[1] * hot_b
    spare = remote(w_h, w_c, wc_s.at[0], wc_r.at[0], z_peer(4))
    spare.start()
    w_n[...] = w[0] * hot_b + w[1] * cold_b

    row = lax.broadcasted_iota(jnp.int32, (TOK, 1), 0)
    outer = jnp.zeros((TOK, 1), jnp.int32)
    for k in range(1, 8):
        outer = outer + jnp.where(row >= k * MOST, 1, 0)
    moved = outer * TOK + row - outer * MOST
    col = lax.broadcasted_iota(jnp.int32, (TOK, 2 * HALF), 1)
    for k in range(8):
        perm[k * TOK : (k + 1) * TOK] = jnp.where(col == moved + k * MOST, 1.0, 0.0).astype(BF)
    for k in range(8):
        perm_h[k * BLOCK : (k + 1) * BLOCK] = perm[k * TOK : k * TOK + BLOCK, 0:HALF]

    loads[1].wait()
    loads[2].wait()

    def forward_n(i, carry):
        at = pl.ds(pl.multiple_of(i * 256, 256), 256)
        rows = hid[0, at] * hot_b + hid[1, at] * cold_b
        hid_n[at] = rows
        out_n[at] = dot(rows, w_n[...]).astype(BF)
        return carry

    lax.fori_loop(0, 3, forward_n, 0)
    back = []
    for i in range(2):
        part = dot(perm[i * HALF : (i + 1) * HALF], out_n[...]).astype(BF)
        sb_n[4 * i : 4 * i + 4] = part.reshape(4, TOK, COLS)
    for i, d in enumerate((4, 3, -3, 2, -2, 1, -1)):
        copy = remote(sb_n.at[(x + d) % X], back_n.at[(-d) % X], bn_s.at[i], bn_r.at[i], x_peer(d))
        copy.start()
        back.append(copy)
    back_n[0] = sb_n[x]

    def forward_h(i, carry):
        at = pl.ds(pl.multiple_of(i * 128, 128), 128)
        far = pl.ds(pl.multiple_of(h * HALF + i * 128, 128), 128)
        rows = hid[0, far] * cold_b + hid[1, far] * hot_b
        hid_h[at] = rows
        out_h[at] = dot(rows, w_h[...]).astype(BF)
        return carry

    lax.fori_loop(0, 3, forward_h, 0)

    for copy in gather:
        copy.wait()

    def hottest(row_of_z):
        pair = load_ref[pl.ds(pl.multiple_of(row_of_z * X, X), X), :]
        return jnp.where(pair[:, 1:2] > pair[:, 0:1], 1.0, 0.0)

    at_x = lax.broadcasted_iota(jnp.int32, (X, 1), 0)
    far_z = (z + 4) % Z
    hot_here = hottest(z)
    home = (2 * (z * X + at_x)).astype(F32)
    name_n = home + 1.0 - hot_here
    name_h = home + hot_here
    name_c = (2 * (far_z * X + at_x)).astype(F32) + hottest(far_z)
    before = jnp.where(
        lax.broadcasted_iota(jnp.int32, (LANES, LANES), 0) < lax.broadcasted_iota(jnp.int32, (LANES, LANES), 1), 1.0, 0.0
    ).astype(BF)

    def match(facts, name):
        hits = jnp.zeros((X, LANES), F32)
        gates = jnp.zeros((X, LANES), F32)
        for k in range(TOP):
            same = facts[k : k + 1, :] == name
            hits = hits + jnp.where(same, 1.0, 0.0)
            gates = gates + jnp.where(same, 0.0625 * (facts[TOP + k : TOP + k + 1, :] + 1.0), 0.0)
        return hits, gates

    def keys(hits, first):
        places = dot(hits.astype(BF), before)
        return jnp.where(hits > 0.5, places + first, -1.0)

    for i in range(Z):
        hits, gates = match(meta[i], name_n)
        key_n[:, i * LANES : (i + 1) * LANES] = keys(hits, float(i * MOST))
        gate_n[:, i * LANES : (i + 1) * LANES] = gates
    for i in range(4):
        facts = meta[4 * h + i]
        hits, gates = match(facts, name_h)
        key_h[:, i * LANES : (i + 1) * LANES] = keys(hits, float(i * MOST))
        gate_h[:, i * LANES : (i + 1) * LANES] = gates
        hits, gates = match(facts, name_c)
        key_c[:, i * LANES : (i + 1) * LANES] = keys(hits, float(BLOCK + i * MOST))
        gate_c[:, i * LANES : (i + 1) * LANES] = gates

    order = (0, 4, 3, 5, 2, 6, 1, 7)
    places_n = lax.broadcasted_iota(jnp.int32, (TOK, Z * LANES), 0).astype(F32)
    dispatch_n = []
    for group in (order[0:4], order[4:8]):
        for d in group:
            at = pl.ds((x + d) % X, 1)
            i = order.index(d)
            g_n[i * TOK : (i + 1) * TOK] = jnp.where(key_n[at, :] == places_n, gate_n[at, :], 0.0).astype(BF)
        i = order.index(group[0])
        rows = dot(g_n[i * TOK : (i + 4) * TOK], tok[...].reshape(Z * LANES, COLS)).astype(BF)
        send_n[i : i + 4] = rows.reshape(4, TOK, COLS)
        for d in group:
            i = order.index(d)
            if d:
                copy = remote(send_n.at[i], recv_n.at[x], dn_s.at[i - 1], dn_r.at[i - 1], x_peer(d))
                copy.start()
                dispatch_n.append(copy)
            else:
                recv_n[x] = send_n[i]
    places_h = lax.broadcasted_iota(jnp.int32, (TOK, 4 * LANES), 0).astype(F32)
    dispatch_h = []
    for group in (order[0:4], order[4:8]):
        for d in group:
            at = pl.ds((x + d) % X, 1)
            i = order.index(d)
            g_hc[i * TOK : (i + 1) * TOK] = (
                jnp.where(key_h[at, :] == places_h, gate_h[at, :], 0.0)
                + jnp.where(key_c[at, :] == places_h, gate_c[at, :], 0.0)
            ).astype(BF)
        i = order.index(group[0])
        rows = dot(g_hc[i * TOK : (i + 4) * TOK], tok[pl.ds(4 * h, 4)].reshape(4 * LANES, COLS)).astype(BF)
        send_hc[i : i + 4] = rows.reshape(4, TOK, COLS)
        for d in group:
            i = order.index(d)
            if d:
                copy = remote(send_hc.at[i], recv_hc.at[x], dh_s.at[i - 1], dh_r.at[i - 1], x_peer(d))
                copy.start()
                dispatch_h.append(copy)
            else:
                recv_hc[x] = send_hc[i]

    part = dot(perm_h[...], out_h[...]).astype(BF)
    sb_h[...] = part.reshape(X, BLOCK, COLS)
    for i, d in enumerate((4, 3, -3, 2, -2, 1, -1)):
        copy = remote(
            sb_h.at[(x + d) % X], back_hc.at[order.index((-d) % X), pl.ds(0, BLOCK)], bh_s.at[i], bh_r.at[i], x_peer(d)
        )
        copy.start()
        back.append(copy)
    back_hc[0, 0:BLOCK] = sb_h[x]

    def partial(rg, first, count, weight, cxs, cxr, sums, sem):
        def rows_of(core):
            return jnp.concatenate(
                [
                    rg[pl.ds(pl.multiple_of(first + (2 * t + core) * BLOCK, 16), BLOCK), :]
                    for t in range(count)
                ],
                axis=0,
            )

        theirs = rows_of(1 - c)
        copies = []
        for side in range(2):
            part = dot_nt(theirs, weight[side * SIDE : (side + 1) * SIDE, :]).astype(BF)
            cxs[side] = part.reshape(count, BLOCK, SIDE)
            copy = remote(cxs.at[side], cxr.at[side], cx_s.at[sem + side], cx_r.at[sem + side], sibling)
            copy.start()
            copies.append(copy)
        mine = rows_of(c)
        for side in range(2):
            part = dot_nt(mine, weight[side * SIDE : (side + 1) * SIDE, :])
            sums[side] = part.reshape(count, BLOCK, SIDE)
        return copies

    for copy in dispatch_n:
        copy.wait()
    for i in range(2):
        rows = dot(perm[i * HALF : (i + 1) * HALF], recv_n[...].reshape(2 * HALF, COLS)).astype(BF)
        rg_n[i * HALF : (i + 1) * HALF] = rows
    pair_n = partial(rg_n, 0, 8, w_n, cxs_n, cxr_n, sum_n, 0)

    def at_step(side, k):
        return (y - (1 - 2 * side) * (1 + k)) % Y

    def ring_copy(kind, side, k):
        rs, rr = ((rs_n, rr_n), (rs_h, rr_h), (rs_c, rr_c))[kind]
        i = (kind * 2 + side) * RING + k
        return remote(rs.at[side, k], rr.at[side, k], ring_s.at[i], ring_r.at[i], y_peer(1 - 2 * side))

    def block_sum(kind, side, t, k):
        sums, cxr, rr = ((sum_n, cxr_n, rr_n), (sum_h, cxr_h, rr_h), (sum_c, cxr_c, rr_c))[kind]
        total = sums[side, t] + cxr[side, t].astype(F32)
        if k > 0:
            total = total + rr[side, k - 1].astype(F32)
        return total

    def ring_step(kind, k):
        rs = (rs_n, rs_h, rs_c)[kind]
        for side in range(2):
            t = at_step(side, k)

            def go(side=side, t=t):
                if k > 0:
                    ring_copy(kind, side, k - 1).wait_recv()
                rs[side, k] = block_sum(kind, side, t if kind == 0 else t % 4, k).astype(BF)
                ring_copy(kind, side, k).start()

            if kind == 0:
                go()
            else:
                pl.when(t // 4 == h)(go)

    def ring_end(kind):
        for side in range(2):
            for k in range(RING):
                if kind == 0:
                    ring_copy(kind, side, k).wait_send()
                else:

                    @pl.when(at_step(side, k) // 4 == h)
                    def _(side=side, k=k):
                        ring_copy(kind, side, k).wait_send()

    for copy in pair_n:
        copy.wait()
    ring_step(0, 0)

    for copy in dispatch_h:
        copy.wait()
    for i in range(2):
        rows = dot(perm[i * HALF : (i + 1) * HALF], recv_hc[...].reshape(2 * HALF, COLS)).astype(BF)
        rg_hc[i * HALF : (i + 1) * HALF] = rows
    pair_h = partial(rg_hc, 0, 4, w_h, cxs_h, cxr_h, sum_h, 2)
    ring_step(0, 1)
    for copy in pair_h:
        copy.wait()
    ring_step(1, 0)

    spare.wait()
    loads[3].wait()

    def forward_c(i, carry):
        at = pl.ds(pl.multiple_of(i * 128, 128), 128)
        out_c[at] = dot(hid_c[at], w_c[...]).astype(BF)
        return carry

    lax.fori_loop(0, 3, forward_c, 0)
    part = dot(perm_h[...], out_c[...]).astype(BF)
    sb_c[...] = part.reshape(X, BLOCK, COLS)
    for i, d in enumerate((4, 3, -3, 2, -2, 1, -1)):
        copy = remote(
            sb_c.at[(x + d) % X], back_hc.at[order.index((-d) % X), pl.ds(BLOCK, BLOCK)], bc_s.at[i], bc_r.at[i], x_peer(d)
        )
        copy.start()
        back.append(copy)
    back_hc[0, BLOCK:TOK] = sb_c[x]
    pair_c = partial(rg_hc, HALF, 4, w_c, cxs_c, cxr_c, sum_c, 4)
    ring_step(0, 2)
    ring_step(1, 1)
    for copy in pair_c:
        copy.wait()
    ring_step(2, 0)

    scale = 2.0 / TOK

    def weight_part(i):
        at = slice(i * 256, (i + 1) * 256)
        grad_n = scale * dot_tn(hid_n[:, at], rg_n[...])
        grad_h = scale * dot_tn(hid_h[:, at], rg_hc[0:HALF])
        wg[0, at] = (grad_n * hot + grad_h * cold).astype(BF)
        wg[1, at] = (grad_n * cold + grad_h * hot).astype(BF)
        sg[0, at] = (scale * dot_tn(hid_c[:, at], rg_hc[HALF : 2 * HALF])).astype(BF)

    for k in range(4):
        ring_step(0, 3 + k)
        ring_step(1, 2 + k)
        ring_step(2, 1 + k)
        weight_part(k)
    stores = [
        pltpu.make_async_copy(wg, wg_hbm, out_sem.at[0]),
        pltpu.make_async_copy(sg, sg_hbm, out_sem.at[1]),
    ]
    for copy in stores:
        copy.start()

    for copy in back:
        copy.wait()
    ring_step(1, 6)
    ring_step(2, 5)

    def combine(i):
        at = slice(i * LANES, (i + 1) * LANES)
        return dot_tn(g_n[:, at], back_n_rows())

    def back_n_rows():
        return jnp.concatenate([back_n[d] for d in order], axis=0)

    total = dot_tn(g_n[...], back_n_rows()).reshape(Z, LANES, COLS)
    mix_s[...] = total[:, 0:TOK]
    near = dot_tn(g_hc[...], back_hc[...].reshape(X * TOK, COLS)).reshape(4, LANES, COLS)
    mix_s[pl.ds(4 * h, 4)] = mix_s[pl.ds(4 * h, 4)] + near[:, 0:TOK]
    mix = []
    for i, d in enumerate((4, 3, -3, 2, -2, 1, -1)):
        mix_r[8 + i] = mix_s[(z + d) % Z].astype(BF)
        copy = remote(mix_r.at[8 + i], mix_r.at[i], mx_s.at[i], mx_r.at[i], z_peer(d))
        copy.start()
        mix.append(copy)
    ring_step(2, 6)

    val_h[...] = jnp.zeros_like(val_h)
    val_c[...] = jnp.zeros_like(val_c)
    value_n = []
    for side in range(2):
        ring_copy(0, side, RING - 1).wait_recv()
        value_n.append(block_sum(0, side, y, RING))

    @pl.when(y // 4 == h)
    def _():
        for side in range(2):
            at = slice(side * SIDE, (side + 1) * SIDE)
            ring_copy(1, side, RING - 1).wait_recv()
            val_h[:, at] = block_sum(1, side, y % 4, RING)
            ring_copy(2, side, RING - 1).wait_recv()
            val_c[:, at] = block_sum(2, side, y % 4, RING)

    for side in range(2):
        at = slice(side * SIDE, (side + 1) * SIDE)
        hg_ref[0, :, at] = (value_n[side] * hot + val_h[:, at] * cold).astype(BF)
        hg_ref[1, :, at] = (value_n[side] * cold + val_h[:, at] * hot).astype(BF)
    hg_ref[2] = val_c[...].astype(BF)

    total = mix_s[z].astype(BF).astype(F32)
    for copy in mix:
        copy.wait()
    for i in range(Z - 1):
        total = total + mix_r[i].astype(F32)
    mixed_ref[...] = total.astype(BF)

    for kind in range(3):
        ring_end(kind)
    for copy in stores:
        copy.wait()


def body(expert_hidden, down_weight, out_grad, expert_ids, gate_code, expert_load):
    vmem = pl.BlockSpec(memory_space=pltpu.VMEM)
    anywhere = pl.BlockSpec(memory_space=pl.ANY)
    dma = pltpu.SemaphoreType.DMA

    def b(*shape):
        return pltpu.VMEM(shape, BF)

    def f(*shape):
        return pltpu.VMEM(shape, F32)

    scratch = [
        b(2, 2 * HALF, H), b(2 * HALF, H), b(HALF, H), b(HALF, H),
        b(2, H, COLS), b(H, COLS), b(H, COLS), b(H, COLS),
        f(LANES, LANES), f(Z, 2 * TOP, LANES), b(Z, LANES, COLS), b(2 * HALF, 2 * HALF), b(HALF, HALF),
        f(X, Z * LANES), f(X, 4 * LANES), f(X, 4 * LANES), f(X, Z * LANES), f(X, 4 * LANES), f(X, 4 * LANES),
        b(X * TOK, Z * LANES), b(X * TOK, 4 * LANES),
        b(2 * HALF, COLS), b(HALF, COLS), b(HALF, COLS),
        b(X, TOK, COLS), b(X, TOK, COLS), b(X, TOK, COLS), b(X, TOK, COLS),
        b(X, TOK, COLS), b(X, BLOCK, COLS), b(X, BLOCK, COLS), b(X, TOK, COLS), b(X, TOK, COLS),
        b(2 * HALF, COLS), b(2 * HALF, COLS),
        b(2, 8, BLOCK, SIDE), b(2, 4, BLOCK, SIDE), b(2, 4, BLOCK, SIDE),
        b(2, 8, BLOCK, SIDE), b(2, 4, BLOCK, SIDE), b(2, 4, BLOCK, SIDE),
        f(2, 8, BLOCK, SIDE), f(2, 4, BLOCK, SIDE), f(2, 4, BLOCK, SIDE),
        b(2, RING, BLOCK, SIDE), b(2, RING, BLOCK, SIDE), b(2, RING, BLOCK, SIDE),
        b(2, RING, BLOCK, SIDE), b(2, RING, BLOCK, SIDE), b(2, RING, BLOCK, SIDE),
        f(Z, TOK, COLS), b(2 * Z, TOK, COLS), f(BLOCK, H), f(BLOCK, H), b(2, H, COLS), b(1, H, COLS),
        dma((4,)), dma((7,)), dma((7,)), dma((7,)), dma((7,)), dma((1,)), dma((1,)),
        dma((7,)), dma((7,)), dma((7,)), dma((7,)), dma((7,)), dma((7,)), dma((7,)), dma((7,)), dma((7,)), dma((7,)),
        dma((6,)), dma((6,)), dma((6 * RING,)), dma((6 * RING,)), dma((7,)), dma((7,)), dma((2,)),
    ]
    return pl.pallas_call(
        kernel,
        out_shape=(
            jax.ShapeDtypeStruct((TOK, COLS), BF),
            jax.ShapeDtypeStruct((3, BLOCK, H), BF),
            jax.ShapeDtypeStruct((2, H, COLS), BF),
            jax.ShapeDtypeStruct((1, H, COLS), BF),
        ),
        in_specs=[anywhere, anywhere, vmem, vmem, vmem, vmem],
        out_specs=(vmem, vmem, anywhere, anywhere),
        scratch_shapes=scratch,
        compiler_params=pltpu.CompilerParams(
            collective_id=0, has_side_effects=True, vmem_limit_bytes=58 * 1024 * 1024
        ),
        name="experts",
    )(expert_hidden, down_weight, out_grad, expert_ids, gate_code, expert_load.reshape(64, 2))


def solution(mesh):
    placed = (
        P("expert", None, None),
        P("expert", None, "dp"),
        P("expert", "dp"),
        P("expert", None),
        P("expert", None),
        P(),
    )
    return jax.shard_map(
        body,
        mesh=mesh,
        in_specs=placed,
        out_specs=(
            P("expert", "dp"),
            P("expert", "dp", None),
            P("expert", None, "dp"),
            P("expert", None, "dp"),
        ),
        check_vma=False,
    )
```

time: 226 us -> 124 us (0.55)
  Pallas kernels: 0 us -> 109 us
  waiting for transfers between devices: 83.1 us -> 0 us
  local copies, waits for them, and re-layouts: 68.3 us -> 13.8 us
  starting transfers between devices: 40.6 us -> 0 us
  between operations: 16.2 us -> 0.64 us
  matrix products: 12.7 us -> 0 us
  other arithmetic: 3.8 us -> 0 us
    pallas_call x0 -> x1, Pallas kernels: none -> 109 us  [body(): pl.pallas_call(kernel, out_shape=(jax.ShapeDtypeStruct((TOK, COLS), BF),...]
    all_to_all x2 -> x0, waiting for transfers between devices: 64.4 us -> none  [the longest x1 33.8 us: body(): lax.all_to_all(outputs.reshape(slot_count, members, capacity, columns), '...]
    scatter x2 -> x0, local copies, waits for them, and re-layouts: 50 us -> none  [body(): outgoing = outgoing.at[dest_slot, target, place].set(grad_rows)]
    all_to_all x2 -> x0, starting transfers between devices: 33.2 us -> none  [the longest x1 22.6 us: body(): lax.all_to_all(outgoing, 'expert', split_axis=1, concat_axis=1, tiled=True)]
    ppermute x1 -> x0, waiting for transfers between devices: 16.4 us -> none  [partner(): lax.ppermute(array, axis, [(i, i ^ 1 << apart) for i in range(lax.axis_si...]
    dot_general x3 -> x0, matrix products: 12.7 us -> none  [the longest x1 4.84 us: body(): jnp.einsum('srd,shd->srh', arrived, slot_weights, preferred_element_type=...]
    ppermute x1 -> x0, starting transfers between devices: 7.41 us -> none  [partner(): lax.ppermute(array, axis, [(i, i ^ 1 << apart) for i in range(lax.axis_si...]
    unnamed x8 -> x5, local copies, waits for them, and re-layouts: 1.17 us -> 8.16 us
  transfers between devices with their start and end apart: 4 -> 0, of which waited for: 4 -> 0; matrix products, arithmetic and copies ran while one was open for 10% -> 0% of each run, Pallas kernels for 0% -> 0%
where the time goes in v1:
time: 124 us; the launch traced here: 123 us
  Pallas kernels  109 us (88%)
  local copies, waits for them, and re-layouts  13.8 us (11%)
    pallas_call x1, Pallas kernels, body(): pl.pallas_call(kernel, out_shape=(jax.ShapeDtypeStruct((TOK, COLS), BF),...  109 us
    unnamed x5, local copies, waits for them, and re-layouts  8.16 us
    pallas_call x2, local copies, waits for them, and re-layouts, body(): pl.pallas_call(kernel, out_shape=(jax.ShapeDtypeStruct((TOK, COLS), BF),...  4.23 us

profile of v1, /device:TPU:14, one launch (start us, length us, event | category | flops | bytes accessed | tf_op | source)
XLA Modules:
  0.0 123.1 jit_solution(16912934045993889410)
XLA Ops:
  0.6 1.4 %reshape.11.load_ref = s32[64,2]{1,0:T(8,128)} reshape(s32[128]{0:T(128)} %param.11) | data formatting | bytes 1024 | tf_op jit(solution)/shard_map/reshape | solution.py:499
  2.0 1.4 %copy.16.ids_ref = s32[96,8]{1,0:T(8,128)} copy(s32[96,8]{0,1:T(8,128)} %param.9) | data formatting | bytes 6144 | tf_op args[3]
  3.4 1.4 %copy.17.code_ref = s32[96,8]{1,0:T(8,128)} copy(s32[96,8]{0,1:T(8,128)} %param.10) | data formatting | bytes 6144 | tf_op args[4]
  4.8 2.3 %copy.15.w_hbm = bf16[2,1024,224]{2,1,0:T(8,128)(2,1)} copy(bf16[2,1024,224]{1,2,0:T(8,128)(2,1)} %param.7) | data formatting | bytes 1835008 | tf_op args[1]
  7.1 108.6 %experts.1 = (bf16[96,224]{1,0:T(8,128)(2,1)}, bf16[3,48,1024]{2,1,0:T(8,128)(2,1)}, bf16[2,1024,224]{2,1,0:T(8,128)(2,1)}, bf16[1,1024,224]{2,1,0:T(8,128)(2,1)}) custom-call(bf16[3,768,1024]{2,1,0:T(8,128)(2,1)} %hid_hbm.1, bf16[2,1024,224]{2,1,0:T(8,128)(2,1)} %copy.15.w_hbm, bf16[96,224]{1,0:T(8,128)(2,1)} %og_ref.1, s32[96,8]{1,0:T(8,128)} %copy.16.ids_ref, ...), custom_call_target="tpu_custom_call" | custom-call | tf_op jit(solution)/shard_map/experts/pallas_call | solution.py:484
  115.7 2.0 %copy.19 = bf16[1,1024,224]{1,2,0:T(8,128)(2,1)} copy(bf16[1,1024,224]{2,1,0:T(8,128)(2,1)} %get-tuple-element.11) | data formatting | bytes 917504 | tf_op jit(solution)/shard_map/experts/pallas_call | solution.py:484
  117.7 2.2 %copy.18 = bf16[2,1024,224]{1,2,0:T(8,128)(2,1)} copy(bf16[2,1024,224]{2,1,0:T(8,128)(2,1)} %get-tuple-element.10) | data formatting | bytes 1835008 | tf_op jit(solution)/shard_map/experts/pallas_call | solution.py:484
  120.0 1.4 %copy.22 = bf16[96,224]{1,0:T(8,128)(2,1)} copy(bf16[96,224]{1,0:T(8,128)(2,1)} %get-tuple-element.16) | data formatting | bytes 86016
  121.4 1.7 %copy.23 = bf16[3,48,1024]{2,1,0:T(8,128)(2,1)} copy(bf16[3,48,1024]{2,1,0:T(8,128)(2,1)} %get-tuple-element.17) | data formatting | bytes 589824

commit v2 on v1

--- a/solution.py
+++ b/solution.py
@@ -40,10 +40,10 @@
     hid_hbm, w_hbm, og_ref, ids_ref, code_ref, load_ref,
     mixed_ref, hg_ref, wg_hbm, sg_hbm,
     hid, hid_n, hid_h, hid_c, w, w_n, w_h, w_c,
-    turn, meta, tok, perm, perm_h,
-    key_n, key_h, key_c, gate_n, gate_h, gate_c, g_n, g_hc,
+    meta, tok, perm, perm_h,
+    key_n, key_h, key_c, gate_n, gate_h, gate_c, g_n, g_hc, gt_n, gt_hc,
     out_n, out_h, out_c, send_n, send_hc, recv_n, recv_hc,
-    sb_n, sb_h, sb_c, back_n, back_hc, rg_n, rg_hc,
+    sb_n, sb_h, sb_c, back_n, back_hc, rg_n, rg_hc, rgt_n, rgt_hc,
     cxs_n, cxs_h, cxs_c, cxr_n, cxr_h, cxr_c, sum_n, sum_h, sum_c,
     rs_n, rs_h, rs_c, rr_n, rr_h, rr_c,
     mix_s, mix_r, val_h, val_c, wg, sg,
@@ -89,10 +89,9 @@
     for peer in peers:
         pl.semaphore_signal(barrier, inc=1, device_id=peer, device_id_type=MESH)
 
-    turn[...] = jnp.full((LANES, LANES), -1.0, F32)
-    turn[0:TOK, 0:TOP] = ids_ref[...].astype(F32)
-    turn[0:TOK, TOP : 2 * TOP] = code_ref[...].astype(F32)
-    meta[z] = turn[...].T[0 : 2 * TOP]
+    meta[z] = jnp.full((2 * TOP, LANES), -1.0, BF)
+    facts = jnp.concatenate([ids_ref[...].astype(F32), code_ref[...].astype(F32)], axis=0)
+    meta[z, :, 0:TOK] = facts.astype(BF)
     tok[z, 0:TOK] = og_ref[...]
     for i in range(Z):
         tok[i, TOK:LANES] = jnp.zeros((LANES - TOK, COLS), BF)
@@ -108,15 +107,23 @@
     for copy in gather:
         copy.start()
 
-    own = load_ref[pl.ds(e, 1), :]
-    hot = jnp.where(own[:, 1:2] > own[:, 0:1], 1.0, 0.0)
+    lane = lax.broadcasted_iota(jnp.int32, (X, LANES), 1)
+    at_x = lax.broadcasted_iota(jnp.int32, (X, 1), 0)
+    loads_all = jnp.broadcast_to(load_ref[...].astype(F32), (X, LANES))
+
+    def hottest(row_of_z):
+        first = 2 * (row_of_z * X + at_x)
+        even = jnp.sum(jnp.where(lane == first, loads_all, 0.0), axis=1, keepdims=True)
+        odd = jnp.sum(jnp.where(lane == first + 1, loads_all, 0.0), axis=1, keepdims=True)
+        return jnp.where(odd > even, 1.0, 0.0)
+
+    hot_here = hottest(z)
+    hot = jnp.sum(jnp.where(at_x == x, hot_here, 0.0), axis=0, keepdims=True)
     hot_b, cold_b = hot.astype(BF), (1.0 - hot).astype(BF)
     cold = 1.0 - hot
 
     loads[0].wait()
     w_h[...] = w[0] * cold_b + w[1] * hot_b
-    spare = remote(w_h, w_c, wc_s.at[0], wc_r.at[0], z_peer(4))
-    spare.start()
     w_n[...] = w[0] * hot_b + w[1] * cold_b
 
     row = lax.broadcasted_iota(jnp.int32, (TOK, 1), 0)
@@ -137,7 +144,7 @@
         at = pl.ds(pl.multiple_of(i * 256, 256), 256)
         rows = hid[0, at] * hot_b + hid[1, at] * cold_b
         hid_n[at] = rows
-        out_n[at] = dot(rows, w_n[...]).astype(BF)
+        out_n[at] = dot_nt(rows, w_n[...]).astype(BF)
         return carry
 
     lax.fori_loop(0, 3, forward_n, 0)
@@ -151,26 +158,12 @@
         back.append(copy)
     back_n[0] = sb_n[x]
 
-    def forward_h(i, carry):
-        at = pl.ds(pl.multiple_of(i * 128, 128), 128)
-        far = pl.ds(pl.multiple_of(h * HALF + i * 128, 128), 128)
-        rows = hid[0, far] * cold_b + hid[1, far] * hot_b
-        hid_h[at] = rows
-        out_h[at] = dot(rows, w_h[...]).astype(BF)
-        return carry
-
-    lax.fori_loop(0, 3, forward_h, 0)
-
     for copy in gather:
         copy.wait()
-
-    def hottest(row_of_z):
-        pair = load_ref[pl.ds(pl.multiple_of(row_of_z * X, X), X), :]
-        return jnp.where(pair[:, 1:2] > pair[:, 0:1], 1.0, 0.0)
-
-    at_x = lax.broadcasted_iota(jnp.int32, (X, 1), 0)
+    spare = remote(w_h, w_c, wc_s.at[0], wc_r.at[0], z_peer(4))
+    spare.start()
+
     far_z = (z + 4) % Z
-    hot_here = hottest(z)
     home = (2 * (z * X + at_x)).astype(F32)
     name_n = home + 1.0 - hot_here
     name_h = home + hot_here
@@ -193,11 +186,11 @@
         return jnp.where(hits > 0.5, places + first, -1.0)
 
     for i in range(Z):
-        hits, gates = match(meta[i], name_n)
+        hits, gates = match(meta[i].astype(F32), name_n)
         key_n[:, i * LANES : (i + 1) * LANES] = keys(hits, float(i * MOST))
         gate_n[:, i * LANES : (i + 1) * LANES] = gates
     for i in range(4):
-        facts = meta[4 * h + i]
+        facts = meta[4 * h + i].astype(F32)
         hits, gates = match(facts, name_h)
         key_h[:, i * LANES : (i + 1) * LANES] = keys(hits, float(i * MOST))
         gate_h[:, i * LANES : (i + 1) * LANES] = gates
@@ -246,15 +239,24 @@
             else:
                 recv_hc[x] = send_hc[i]
 
+    def forward_h(i, carry):
+        at = pl.ds(pl.multiple_of(i * 128, 128), 128)
+        far = pl.ds(pl.multiple_of(h * HALF + i * 128, 128), 128)
+        rows = hid[0, far] * cold_b + hid[1, far] * hot_b
+        hid_h[at] = rows
+        out_h[at] = dot_nt(rows, w_h[...]).astype(BF)
+        return carry
+
+    lax.fori_loop(0, 3, forward_h, 0)
+
     part = dot(perm_h[...], out_h[...]).astype(BF)
     sb_h[...] = part.reshape(X, BLOCK, COLS)
-    for i, d in enumerate((4, 3, -3, 2, -2, 1, -1)):
-        copy = remote(
-            sb_h.at[(x + d) % X], back_hc.at[order.index((-d) % X), pl.ds(0, BLOCK)], bh_s.at[i], bh_r.at[i], x_peer(d)
-        )
-        copy.start()
-        back.append(copy)
-    back_hc[0, 0:BLOCK] = sb_h[x]
+    for i in range(4):
+        at = slice(i * 2 * LANES, (i + 1) * 2 * LANES)
+        gt_n[at] = g_n[:, at].T
+    for i in range(2):
+        at = slice(i * 2 * LANES, (i + 1) * 2 * LANES)
+        gt_hc[at] = g_hc[:, at].T
 
     def partial(rg, first, count, weight, cxs, cxr, sums, sem):
         def rows_of(core):
@@ -269,14 +271,14 @@
         theirs = rows_of(1 - c)
         copies = []
         for side in range(2):
-            part = dot_nt(theirs, weight[side * SIDE : (side + 1) * SIDE, :]).astype(BF)
+            part = dot(theirs, weight[:, side * SIDE : (side + 1) * SIDE]).astype(BF)
             cxs[side] = part.reshape(count, BLOCK, SIDE)
             copy = remote(cxs.at[side], cxr.at[side], cx_s.at[sem + side], cx_r.at[sem + side], sibling)
             copy.start()
             copies.append(copy)
         mine = rows_of(c)
         for side in range(2):
-            part = dot_nt(mine, weight[side * SIDE : (side + 1) * SIDE, :])
+            part = dot(mine, weight[:, side * SIDE : (side + 1) * SIDE])
             sums[side] = part.reshape(count, BLOCK, SIDE)
         return copies
 
@@ -329,9 +331,18 @@
                     def _(side=side, k=k):
                         ring_copy(kind, side, k).wait_send()
 
+    for i, d in enumerate((4, 3, -3, 2, -2, 1, -1)):
+        copy = remote(
+            sb_h.at[(x + d) % X], back_hc.at[order.index((-d) % X), pl.ds(0, BLOCK)], bh_s.at[i], bh_r.at[i], x_peer(d)
+        )
+        copy.start()
+        back.append(copy)
+    back_hc[0, 0:BLOCK] = sb_h[x]
+
     for copy in pair_n:
         copy.wait()
     ring_step(0, 0)
+    ring_step(0, 1)
 
     for copy in dispatch_h:
         copy.wait()
@@ -339,17 +350,19 @@
         rows = dot(perm[i * HALF : (i + 1) * HALF], recv_hc[...].reshape(2 * HALF, COLS)).astype(BF)
         rg_hc[i * HALF : (i + 1) * HALF] = rows
     pair_h = partial(rg_hc, 0, 4, w_h, cxs_h, cxr_h, sum_h, 2)
-    ring_step(0, 1)
+    ring_step(0, 2)
     for copy in pair_h:
         copy.wait()
     ring_step(1, 0)
+    ring_step(0, 3)
+    ring_step(1, 1)
 
     spare.wait()
     loads[3].wait()
 
     def forward_c(i, carry):
         at = pl.ds(pl.multiple_of(i * 128, 128), 128)
-        out_c[at] = dot(hid_c[at], w_c[...]).astype(BF)
+        out_c[at] = dot_nt(hid_c[at], w_c[...]).astype(BF)
         return carry
 
     lax.fori_loop(0, 3, forward_c, 0)
@@ -363,56 +376,60 @@
         back.append(copy)
     back_hc[0, BLOCK:TOK] = sb_c[x]
     pair_c = partial(rg_hc, HALF, 4, w_c, cxs_c, cxr_c, sum_c, 4)
-    ring_step(0, 2)
-    ring_step(1, 1)
+    ring_step(0, 4)
+    ring_step(1, 2)
     for copy in pair_c:
         copy.wait()
     ring_step(2, 0)
 
     scale = 2.0 / TOK
 
+    def turn_rows():
+        rgt_n[...] = rg_n[...].T
+        rgt_hc[...] = rg_hc[...].T
+
     def weight_part(i):
-        at = slice(i * 256, (i + 1) * 256)
-        grad_n = scale * dot_tn(hid_n[:, at], rg_n[...])
-        grad_h = scale * dot_tn(hid_h[:, at], rg_hc[0:HALF])
-        wg[0, at] = (grad_n * hot + grad_h * cold).astype(BF)
-        wg[1, at] = (grad_n * cold + grad_h * hot).astype(BF)
-        sg[0, at] = (scale * dot_tn(hid_c[:, at], rg_hc[HALF : 2 * HALF])).astype(BF)
-
-    for k in range(4):
-        ring_step(0, 3 + k)
-        ring_step(1, 2 + k)
-        ring_step(2, 1 + k)
-        weight_part(k)
+        at = slice(i * SIDE, (i + 1) * SIDE)
+        grad_n = scale * dot(rgt_n[...], hid_n[:, at])
+        grad_h = scale * dot(rgt_hc[:, 0:HALF], hid_h[:, at])
+        wg[0, :, at] = (grad_n * hot + grad_h * cold).astype(BF)
+        wg[1, :, at] = (grad_n * cold + grad_h * hot).astype(BF)
+        sg[0, :, at] = (scale * dot(rgt_hc[:, HALF : 2 * HALF], hid_c[:, at])).astype(BF)
+
+    turn_rows()
+    ring_step(0, 5)
+    ring_step(1, 3)
+    ring_step(2, 1)
+    for copy in back[0:7]:
+        copy.wait()
+    rows = jnp.concatenate([back_n[d] for d in order], axis=0)
+    mix_s[...] = dot(gt_n[...], rows).reshape(Z, LANES, COLS)[:, 0:TOK]
+    ring_step(0, 6)
+    ring_step(1, 4)
+    ring_step(2, 2)
+    for copy in back[7:]:
+        copy.wait()
+    near = dot(gt_hc[...], back_hc[...].reshape(X * TOK, COLS)).reshape(4, LANES, COLS)
+    mix_s[pl.ds(4 * h, 4)] = mix_s[pl.ds(4 * h, 4)] + near[:, 0:TOK]
+    mix = []
+    for i, d in enumerate((4, 3, -3, 2, -2, 1, -1)):
+        mix_r[8 + i] = mix_s[(z + d) % Z].astype(BF)
+        copy = remote(mix_r.at[8 + i], mix_r.at[i], mx_s.at[i], mx_r.at[i], z_peer(d))
+        copy.start()
+        mix.append(copy)
+    ring_step(1, 5)
+    ring_step(2, 3)
+    weight_part(0)
+    ring_step(1, 6)
+    ring_step(2, 4)
+    weight_part(1)
     stores = [
         pltpu.make_async_copy(wg, wg_hbm, out_sem.at[0]),
         pltpu.make_async_copy(sg, sg_hbm, out_sem.at[1]),
     ]
     for copy in stores:
         copy.start()
-
-    for copy in back:
-        copy.wait()
-    ring_step(1, 6)
     ring_step(2, 5)
-
-    def combine(i):
-        at = slice(i * LANES, (i + 1) * LANES)
-        return dot_tn(g_n[:, at], back_n_rows())
-
-    def back_n_rows():
-        return jnp.concatenate([back_n[d] for d in order], axis=0)
-
-    total = dot_tn(g_n[...], back_n_rows()).reshape(Z, LANES, COLS)
-    mix_s[...] = total[:, 0:TOK]
-    near = dot_tn(g_hc[...], back_hc[...].reshape(X * TOK, COLS)).reshape(4, LANES, COLS)
-    mix_s[pl.ds(4 * h, 4)] = mix_s[pl.ds(4 * h, 4)] + near[:, 0:TOK]
-    mix = []
-    for i, d in enumerate((4, 3, -3, 2, -2, 1, -1)):
-        mix_r[8 + i] = mix_s[(z + d) % Z].astype(BF)
-        copy = remote(mix_r.at[8 + i], mix_r.at[i], mx_s.at[i], mx_r.at[i], z_peer(d))
-        copy.start()
-        mix.append(copy)
     ring_step(2, 6)
 
     val_h[...] = jnp.zeros_like(val_h)
@@ -437,7 +454,7 @@
         hg_ref[1, :, at] = (value_n[side] * cold + val_h[:, at] * hot).astype(BF)
     hg_ref[2] = val_c[...].astype(BF)
 
-    total = mix_s[z].astype(BF).astype(F32)
+    total = mix_s[z]
     for copy in mix:
         copy.wait()
     for i in range(Z - 1):
@@ -447,6 +464,15 @@
     for kind in range(3):
         ring_end(kind)
     for copy in stores:
+        copy.wait()
+
+
+def store(*refs):
+    sem = refs[8]
+    copies = [pltpu.make_async_copy(refs[i], refs[4 + i], sem.at[i]) for i in range(4)]
+    for copy in copies:
+        copy.start()
+    for copy in copies:
         copy.wait()
 
 
@@ -463,32 +489,33 @@
 
     scratch = [
         b(2, 2 * HALF, H), b(2 * HALF, H), b(HALF, H), b(HALF, H),
-        b(2, H, COLS), b(H, COLS), b(H, COLS), b(H, COLS),
-        f(LANES, LANES), f(Z, 2 * TOP, LANES), b(Z, LANES, COLS), b(2 * HALF, 2 * HALF), b(HALF, HALF),
+        b(2, COLS, H), b(COLS, H), b(COLS, H), b(COLS, H),
+        b(Z, 2 * TOP, LANES), b(Z, LANES, COLS), b(2 * HALF, 2 * HALF), b(HALF, HALF),
         f(X, Z * LANES), f(X, 4 * LANES), f(X, 4 * LANES), f(X, Z * LANES), f(X, 4 * LANES), f(X, 4 * LANES),
-        b(X * TOK, Z * LANES), b(X * TOK, 4 * LANES),
+        b(X * TOK, Z * LANES), b(X * TOK, 4 * LANES), b(Z * LANES, X * TOK), b(4 * LANES, X * TOK),
         b(2 * HALF, COLS), b(HALF, COLS), b(HALF, COLS),
         b(X, TOK, COLS), b(X, TOK, COLS), b(X, TOK, COLS), b(X, TOK, COLS),
         b(X, TOK, COLS), b(X, BLOCK, COLS), b(X, BLOCK, COLS), b(X, TOK, COLS), b(X, TOK, COLS),
-        b(2 * HALF, COLS), b(2 * HALF, COLS),
+        b(2 * HALF, COLS), b(2 * HALF, COLS), b(COLS, 2 * HALF), b(COLS, 2 * HALF),
         b(2, 8, BLOCK, SIDE), b(2, 4, BLOCK, SIDE), b(2, 4, BLOCK, SIDE),
         b(2, 8, BLOCK, SIDE), b(2, 4, BLOCK, SIDE), b(2, 4, BLOCK, SIDE),
         f(2, 8, BLOCK, SIDE), f(2, 4, BLOCK, SIDE), f(2, 4, BLOCK, SIDE),
         b(2, RING, BLOCK, SIDE), b(2, RING, BLOCK, SIDE), b(2, RING, BLOCK, SIDE),
         b(2, RING, BLOCK, SIDE), b(2, RING, BLOCK, SIDE), b(2, RING, BLOCK, SIDE),
-        f(Z, TOK, COLS), b(2 * Z, TOK, COLS), f(BLOCK, H), f(BLOCK, H), b(2, H, COLS), b(1, H, COLS),
+        f(Z, TOK, COLS), b(2 * Z, TOK, COLS), f(BLOCK, H), f(BLOCK, H), b(2, COLS, H), b(1, COLS, H),
         dma((4,)), dma((7,)), dma((7,)), dma((7,)), dma((7,)), dma((1,)), dma((1,)),
         dma((7,)), dma((7,)), dma((7,)), dma((7,)), dma((7,)), dma((7,)), dma((7,)), dma((7,)), dma((7,)), dma((7,)),
         dma((6,)), dma((6,)), dma((6 * RING,)), dma((6 * RING,)), dma((7,)), dma((7,)), dma((2,)),
     ]
-    return pl.pallas_call(
+    shapes = (
+        jax.ShapeDtypeStruct((TOK, COLS), BF),
+        jax.ShapeDtypeStruct((3, BLOCK, H), BF),
+        jax.ShapeDtypeStruct((2, COLS, H), BF),
+        jax.ShapeDtypeStruct((1, COLS, H), BF),
+    )
+    results = pl.pallas_call(
         kernel,
-        out_shape=(
-            jax.ShapeDtypeStruct((TOK, COLS), BF),
-            jax.ShapeDtypeStruct((3, BLOCK, H), BF),
-            jax.ShapeDtypeStruct((2, H, COLS), BF),
-            jax.ShapeDtypeStruct((1, H, COLS), BF),
-        ),
+        out_shape=shapes,
         in_specs=[anywhere, anywhere, vmem, vmem, vmem, vmem],
         out_specs=(vmem, vmem, anywhere, anywhere),
         scratch_shapes=scratch,
@@ -496,7 +523,23 @@
             collective_id=0, has_side_effects=True, vmem_limit_bytes=58 * 1024 * 1024
         ),
         name="experts",
-    )(expert_hidden, down_weight, out_grad, expert_ids, gate_code, expert_load.reshape(64, 2))
+    )(
+        expert_hidden,
+        jnp.swapaxes(down_weight, 1, 2),
+        out_grad,
+        expert_ids.T,
+        gate_code.T,
+        expert_load.reshape(1, LANES),
+    )
+    mixed, hidden_grad, weight_grad, spare_grad = pl.pallas_call(
+        store,
+        out_shape=shapes,
+        in_specs=[anywhere] * 4,
+        out_specs=[anywhere] * 4,
+        scratch_shapes=[dma((4,))],
+        name="store",
+    )(*results)
+    return mixed, hidden_grad, jnp.swapaxes(weight_grad, 1, 2), jnp.swapaxes(spare_grad, 1, 2)
 
 
 def solution(mesh):

time: 124 us -> 146 us (1.18)
  Pallas kernels: 109 us -> 143 us
  local copies, waits for them, and re-layouts: 13.8 us -> 0 us
    pallas_call x1 -> x2, Pallas kernels: 109 us -> 143 us  [the longest x1 89.8 us: body(): pl.pallas_call(kernel, out_shape=shapes, in_specs=[anywhere, anywhere, vm...]
    unnamed x5 -> x0, local copies, waits for them, and re-layouts: 8.16 us -> none
    pallas_call x2 -> x0, local copies, waits for them, and re-layouts: 4.23 us -> none  [body(): pl.pallas_call(kernel, out_shape=(jax.ShapeDtypeStruct((TOK, COLS), BF),...]
where the time goes in v2:
time: 146 us; the launch traced here: 144 us
  Pallas kernels  143 us (98%)
    pallas_call x1, Pallas kernels, body(): pl.pallas_call(kernel, out_shape=shapes, in_specs=[anywhere, anywhere, vm...  89.8 us
    pallas_call x1, Pallas kernels, body(): pl.pallas_call(store, out_shape=shapes, in_specs=[anywhere] * 4, out_spec...  53.3 us

profile of v2, /device:TPU:14, one launch (start us, length us, event | category | flops | bytes accessed | tf_op | source)
XLA Modules:
  0.0 143.7 jit_solution(11872795422461463414)
XLA Ops:
  0.6 89.8 %experts.1 = (bf16[96,224]{1,0:T(8,128)(2,1)}, bf16[3,48,1024]{2,1,0:T(8,128)(2,1)}, bf16[2,224,1024]{2,1,0:T(8,128)(2,1)}, bf16[1,224,1024]{2,1,0:T(8,128)(2,1)}) custom-call(bf16[3,768,1024]{2,1,0:T(8,128)(2,1)} %hid_hbm.1, bf16[2,224,1024]{2,1,0:T(8,128)(2,1)} %bitcast.6, bf16[96,224]{1,0:T(8,128)(2,1)} %og_ref.1, s32[8,96]{1,0:T(8,128)} %bitcast.7, ...), custom_call_target="tpu_custom_call" | custom-call | tf_op jit(solution)/shard_map/experts/pallas_call | solution.py:516
  90.4 53.3 %store.1 = (bf16[96,224]{1,0:T(8,128)(2,1)}, bf16[3,48,1024]{2,1,0:T(8,128)(2,1)}, bf16[2,224,1024]{2,1,0:T(8,128)(2,1)}, bf16[1,224,1024]{2,1,0:T(8,128)(2,1)}) custom-call(bf16[96,224]{1,0:T(8,128)(2,1)} %get-tuple-element.12.refs_0_, bf16[3,48,1024]{2,1,0:T(8,128)(2,1)} %get-tuple-element.13.refs_1_, bf16[2,224,1024]{2,1,0:T(8,128)(2,1)} %get-tuple-element.14.refs_2_, ...), custom_call_target="tpu_custom_call" | custom-call | tf_op jit(solution)/shard_map/store/pallas_call | solution.py:534

commit v3 on v2

--- a/solution.py
+++ b/solution.py
@@ -468,12 +468,16 @@
 
 
 def store(*refs):
-    sem = refs[8]
-    copies = [pltpu.make_async_copy(refs[i], refs[4 + i], sem.at[i]) for i in range(4)]
-    for copy in copies:
-        copy.start()
-    for copy in copies:
-        copy.wait()
+    given, results, held, sem = refs[0:4], refs[4:8], refs[8:12], refs[12]
+    inward = [pltpu.make_async_copy(given[i], held[i], sem.at[i]) for i in range(4)]
+    outward = [pltpu.make_async_copy(held[i], results[i], sem.at[4 + i]) for i in range(4)]
+    for i in range(4):
+        inward[i].start()
+    for i in range(4):
+        inward[i].wait()
+        outward[i].start()
+    for i in range(4):
+        outward[i].wait()
 
 
 def body(expert_hidden, down_weight, out_grad, expert_ids, gate_code, expert_load):
@@ -536,7 +540,7 @@
         out_shape=shapes,
         in_specs=[anywhere] * 4,
         out_specs=[anywhere] * 4,
-        scratch_shapes=[dma((4,))],
+        scratch_shapes=[b(TOK, COLS), b(3, BLOCK, H), b(2, COLS, H), b(1, COLS, H), dma((8,))],
         name="store",
     )(*results)
     return mixed, hidden_grad, jnp.swapaxes(weight_grad, 1, 2), jnp.swapaxes(spare_grad, 1, 2)

time: 146 us -> 95.2 us (0.65)
  the two profiles are of different devices: /device:TPU:14 before, /device:TPU:16 now
where the time goes in v3:
time: 95.2 us; the launch traced here: 95 us
  Pallas kernels  94.3 us (99%)
    pallas_call x1, Pallas kernels, body(): pl.pallas_call(kernel, out_shape=shapes, in_specs=[anywhere, anywhere, vm...  91.9 us
    pallas_call x1, Pallas kernels, body(): pl.pallas_call(store, out_shape=shapes, in_specs=[anywhere] * 4, out_spec...  2.44 us

profile of v3, /device:TPU:16, one launch (start us, length us, event | category | flops | bytes accessed | tf_op | source)
XLA Modules:
  0.0 95.0 jit_solution(5259123357564742072)
XLA Ops:
  0.6 91.9 %experts.1 = (bf16[96,224]{1,0:T(8,128)(2,1)}, bf16[3,48,1024]{2,1,0:T(8,128)(2,1)}, bf16[2,224,1024]{2,1,0:T(8,128)(2,1)}, bf16[1,224,1024]{2,1,0:T(8,128)(2,1)}) custom-call(bf16[3,768,1024]{2,1,0:T(8,128)(2,1)} %hid_hbm.1, bf16[2,224,1024]{2,1,0:T(8,128)(2,1)} %bitcast.6, bf16[96,224]{1,0:T(8,128)(2,1)} %og_ref.1, s32[8,96]{1,0:T(8,128)} %bitcast.7, ...), custom_call_target="tpu_custom_call" | custom-call | tf_op jit(solution)/shard_map/experts/pallas_call | solution.py:520
  92.5 2.4 %store.1 = (bf16[96,224]{1,0:T(8,128)(2,1)}, bf16[3,48,1024]{2,1,0:T(8,128)(2,1)}, bf16[2,224,1024]{2,1,0:T(8,128)(2,1)}, bf16[1,224,1024]{2,1,0:T(8,128)(2,1)}) custom-call(bf16[96,224]{1,0:T(8,128)(2,1)} %get-tuple-element.12.refs_0_, bf16[3,48,1024]{2,1,0:T(8,128)(2,1)} %get-tuple-element.13.refs_1_, bf16[2,224,1024]{2,1,0:T(8,128)(2,1)} %get-tuple-element.14.refs_2_, ...), custom_call_target="tpu_custom_call" | custom-call | tf_op jit(solution)/shard_map/store/pallas_call | solution.py:538

commit v4 on v3

--- a/solution.py
+++ b/solution.py
@@ -41,15 +41,15 @@
     mixed_ref, hg_ref, wg_hbm, sg_hbm,
     hid, hid_n, hid_h, hid_c, w, w_n, w_h, w_c,
     meta, tok, perm, perm_h,
-    key_n, key_h, key_c, gate_n, gate_h, gate_c, g_n, g_hc, gt_n, gt_hc,
+    key_n, key_h, key_c, gate_n, gate_h, gate_c, g_n, g_hc, gt_n, gt_h, gt_c,
     out_n, out_h, out_c, send_n, send_hc, recv_n, recv_hc,
-    sb_n, sb_h, sb_c, back_n, back_hc, rg_n, rg_hc, rgt_n, rgt_hc,
+    sb_n, sb_h, sb_c, back_n, back_h, back_c, rg_n, rg_hc, rgt_n, rgt_hc,
     cxs_n, cxs_h, cxs_c, cxr_n, cxr_h, cxr_c, sum_n, sum_h, sum_c,
     rs_n, rs_h, rs_c, rr_n, rr_h, rr_c,
-    mix_s, mix_r, val_h, val_c, wg, sg,
+    mix_s, mix_r, mix_c, mixc_r, val_h, val_c, wg, sg,
     load_sem, zt_s, zt_r, zm_s, zm_r, wc_s, wc_r,
     dn_s, dn_r, dh_s, dh_r, bn_s, bn_r, bh_s, bh_r, bc_s, bc_r,
-    cx_s, cx_r, ring_s, ring_r, mx_s, mx_r, out_sem,
+    cx_s, cx_r, ring_s, ring_r, mx_s, mx_r, mxc_s, mxc_r, out_sem,
 ):
     e = lax.axis_index("expert")
     dp = lax.axis_index("dp")
@@ -98,11 +98,14 @@
 
     pl.semaphore_wait(barrier, len(peers))
 
+    near = [4 * h + (z + i) % 4 for i in range(1, 4)]
+    far = [4 * (1 - h) + (z + i) % 4 for i in range(4)]
     gather = []
-    for i, d in enumerate((4, 3, -3, 2, -2, 1, -1)):
-        gather.append(remote(meta.at[z], meta.at[z], zm_s.at[i], zm_r.at[i], z_peer(d)))
+    for i, other in enumerate(near + far):
+        peer = (other * X + x, dp)
+        gather.append(remote(meta.at[z], meta.at[z], zm_s.at[i], zm_r.at[i], peer))
         gather.append(
-            remote(tok.at[z, pl.ds(0, TOK)], tok.at[z, pl.ds(0, TOK)], zt_s.at[i], zt_r.at[i], z_peer(d))
+            remote(tok.at[z, pl.ds(0, TOK)], tok.at[z, pl.ds(0, TOK)], zt_s.at[i], zt_r.at[i], peer)
         )
     for copy in gather:
         copy.start()
@@ -158,7 +161,7 @@
         back.append(copy)
     back_n[0] = sb_n[x]
 
-    for copy in gather:
+    for copy in gather[0:6]:
         copy.wait()
     spare = remote(w_h, w_c, wc_s.at[0], wc_r.at[0], z_peer(4))
     spare.start()
@@ -185,10 +188,6 @@
         places = dot(hits.astype(BF), before)
         return jnp.where(hits > 0.5, places + first, -1.0)
 
-    for i in range(Z):
-        hits, gates = match(meta[i].astype(F32), name_n)
-        key_n[:, i * LANES : (i + 1) * LANES] = keys(hits, float(i * MOST))
-        gate_n[:, i * LANES : (i + 1) * LANES] = gates
     for i in range(4):
         facts = meta[4 * h + i].astype(F32)
         hits, gates = match(facts, name_h)
@@ -199,24 +198,6 @@
         gate_c[:, i * LANES : (i + 1) * LANES] = gates
 
     order = (0, 4, 3, 5, 2, 6, 1, 7)
-    places_n = lax.broadcasted_iota(jnp.int32, (TOK, Z * LANES), 0).astype(F32)
-    dispatch_n = []
-    for group in (order[0:4], order[4:8]):
-        for d in group:
-            at = pl.ds((x + d) % X, 1)
-            i = order.index(d)
-            g_n[i * TOK : (i + 1) * TOK] = jnp.where(key_n[at, :] == places_n, gate_n[at, :], 0.0).astype(BF)
-        i = order.index(group[0])
-        rows = dot(g_n[i * TOK : (i + 4) * TOK], tok[...].reshape(Z * LANES, COLS)).astype(BF)
-        send_n[i : i + 4] = rows.reshape(4, TOK, COLS)
-        for d in group:
-            i = order.index(d)
-            if d:
-                copy = remote(send_n.at[i], recv_n.at[x], dn_s.at[i - 1], dn_r.at[i - 1], x_peer(d))
-                copy.start()
-                dispatch_n.append(copy)
-            else:
-                recv_n[x] = send_n[i]
     places_h = lax.broadcasted_iota(jnp.int32, (TOK, 4 * LANES), 0).astype(F32)
     dispatch_h = []
     for group in (order[0:4], order[4:8]):
@@ -239,6 +220,31 @@
             else:
                 recv_hc[x] = send_hc[i]
 
+    for copy in gather[6:]:
+        copy.wait()
+    for i in range(Z):
+        hits, gates = match(meta[i].astype(F32), name_n)
+        key_n[:, i * LANES : (i + 1) * LANES] = keys(hits, float(i * MOST))
+        gate_n[:, i * LANES : (i + 1) * LANES] = gates
+    places_n = lax.broadcasted_iota(jnp.int32, (TOK, Z * LANES), 0).astype(F32)
+    dispatch_n = []
+    for group in (order[0:4], order[4:8]):
+        for d in group:
+            at = pl.ds((x + d) % X, 1)
+            i = order.index(d)
+            g_n[i * TOK : (i + 1) * TOK] = jnp.where(key_n[at, :] == places_n, gate_n[at, :], 0.0).astype(BF)
+        i = order.index(group[0])
+        rows = dot(g_n[i * TOK : (i + 4) * TOK], tok[...].reshape(Z * LANES, COLS)).astype(BF)
+        send_n[i : i + 4] = rows.reshape(4, TOK, COLS)
+        for d in group:
+            i = order.index(d)
+            if d:
+                copy = remote(send_n.at[i], recv_n.at[x], dn_s.at[i - 1], dn_r.at[i - 1], x_peer(d))
+                copy.start()
+                dispatch_n.append(copy)
+            else:
+                recv_n[x] = send_n[i]
+
     def forward_h(i, carry):
         at = pl.ds(pl.multiple_of(i * 128, 128), 128)
         far = pl.ds(pl.multiple_of(h * HALF + i * 128, 128), 128)
@@ -256,7 +262,9 @@
         gt_n[at] = g_n[:, at].T
     for i in range(2):
         at = slice(i * 2 * LANES, (i + 1) * 2 * LANES)
-        gt_hc[at] = g_hc[:, at].T
+        both = g_hc[:, at].reshape(X, TOK, 2 * LANES)
+        gt_h[at] = both[:, 0:BLOCK].reshape(HALF, 2 * LANES).T
+        gt_c[at] = both[:, BLOCK:TOK].reshape(HALF, 2 * LANES).T
 
     def partial(rg, first, count, weight, cxs, cxr, sums, sem):
         def rows_of(core):
@@ -282,13 +290,6 @@
             sums[side] = part.reshape(count, BLOCK, SIDE)
         return copies
 
-    for copy in dispatch_n:
-        copy.wait()
-    for i in range(2):
-        rows = dot(perm[i * HALF : (i + 1) * HALF], recv_n[...].reshape(2 * HALF, COLS)).astype(BF)
-        rg_n[i * HALF : (i + 1) * HALF] = rows
-    pair_n = partial(rg_n, 0, 8, w_n, cxs_n, cxr_n, sum_n, 0)
-
     def at_step(side, k):
         return (y - (1 - 2 * side) * (1 + k)) % Y
 
@@ -331,31 +332,33 @@
                     def _(side=side, k=k):
                         ring_copy(kind, side, k).wait_send()
 
-    for i, d in enumerate((4, 3, -3, 2, -2, 1, -1)):
-        copy = remote(
-            sb_h.at[(x + d) % X], back_hc.at[order.index((-d) % X), pl.ds(0, BLOCK)], bh_s.at[i], bh_r.at[i], x_peer(d)
-        )
-        copy.start()
-        back.append(copy)
-    back_hc[0, 0:BLOCK] = sb_h[x]
-
-    for copy in pair_n:
-        copy.wait()
-    ring_step(0, 0)
-    ring_step(0, 1)
-
     for copy in dispatch_h:
         copy.wait()
     for i in range(2):
         rows = dot(perm[i * HALF : (i + 1) * HALF], recv_hc[...].reshape(2 * HALF, COLS)).astype(BF)
         rg_hc[i * HALF : (i + 1) * HALF] = rows
     pair_h = partial(rg_hc, 0, 4, w_h, cxs_h, cxr_h, sum_h, 2)
-    ring_step(0, 2)
+    for i, d in enumerate((4, 3, -3, 2, -2, 1, -1)):
+        copy = remote(
+            sb_h.at[(x + d) % X], back_h.at[order.index((-d) % X)], bh_s.at[i], bh_r.at[i], x_peer(d)
+        )
+        copy.start()
+        back.append(copy)
+    back_h[0] = sb_h[x]
     for copy in pair_h:
         copy.wait()
     ring_step(1, 0)
-    ring_step(0, 3)
     ring_step(1, 1)
+    for copy in dispatch_n:
+        copy.wait()
+    for i in range(2):
+        rows = dot(perm[i * HALF : (i + 1) * HALF], recv_n[...].reshape(2 * HALF, COLS)).astype(BF)
+        rg_n[i * HALF : (i + 1) * HALF] = rows
+    pair_n = partial(rg_n, 0, 8, w_n, cxs_n, cxr_n, sum_n, 0)
+    ring_step(1, 2)
+    for copy in pair_n:
+        copy.wait()
+    ring_step(0, 0)
 
     spare.wait()
     loads[3].wait()
@@ -370,14 +373,14 @@
     sb_c[...] = part.reshape(X, BLOCK, COLS)
     for i, d in enumerate((4, 3, -3, 2, -2, 1, -1)):
         copy = remote(
-            sb_c.at[(x + d) % X], back_hc.at[order.index((-d) % X), pl.ds(BLOCK, BLOCK)], bc_s.at[i], bc_r.at[i], x_peer(d)
+            sb_c.at[(x + d) % X], back_c.at[order.index((-d) % X)], bc_s.at[i], bc_r.at[i], x_peer(d)
         )
         copy.start()
         back.append(copy)
-    back_hc[0, BLOCK:TOK] = sb_c[x]
+    back_c[0] = sb_c[x]
     pair_c = partial(rg_hc, HALF, 4, w_c, cxs_c, cxr_c, sum_c, 4)
-    ring_step(0, 4)
-    ring_step(1, 2)
+    ring_step(1, 3)
+    ring_step(0, 1)
     for copy in pair_c:
         copy.wait()
     ring_step(2, 0)
@@ -397,31 +400,13 @@
         sg[0, :, at] = (scale * dot(rgt_hc[:, HALF : 2 * HALF], hid_c[:, at])).astype(BF)
 
     turn_rows()
-    ring_step(0, 5)
-    ring_step(1, 3)
+    ring_step(1, 4)
+    ring_step(0, 2)
     ring_step(2, 1)
-    for copy in back[0:7]:
-        copy.wait()
-    rows = jnp.concatenate([back_n[d] for d in order], axis=0)
-    mix_s[...] = dot(gt_n[...], rows).reshape(Z, LANES, COLS)[:, 0:TOK]
-    ring_step(0, 6)
-    ring_step(1, 4)
+    weight_part(0)
+    ring_step(1, 5)
+    ring_step(0, 3)
     ring_step(2, 2)
-    for copy in back[7:]:
-        copy.wait()
-    near = dot(gt_hc[...], back_hc[...].reshape(X * TOK, COLS)).reshape(4, LANES, COLS)
-    mix_s[pl.ds(4 * h, 4)] = mix_s[pl.ds(4 * h, 4)] + near[:, 0:TOK]
-    mix = []
-    for i, d in enumerate((4, 3, -3, 2, -2, 1, -1)):
-        mix_r[8 + i] = mix_s[(z + d) % Z].astype(BF)
-        copy = remote(mix_r.at[8 + i], mix_r.at[i], mx_s.at[i], mx_r.at[i], z_peer(d))
-        copy.start()
-        mix.append(copy)
-    ring_step(1, 5)
-    ring_step(2, 3)
-    weight_part(0)
-    ring_step(1, 6)
-    ring_step(2, 4)
     weight_part(1)
     stores = [
         pltpu.make_async_copy(wg, wg_hbm, out_sem.at[0]),
@@ -429,6 +414,33 @@
     ]
     for copy in stores:
         copy.start()
+    ring_step(1, 6)
+    ring_step(0, 4)
+    ring_step(2, 3)
+
+    for copy in back[0:14]:
+        copy.wait()
+    rows = jnp.concatenate([back_n[d] for d in order], axis=0)
+    mix_s[...] = dot(gt_n[...], rows).reshape(Z, LANES, COLS)[:, 0:TOK]
+    added = dot(gt_h[...], back_h[...].reshape(HALF, COLS)).reshape(4, LANES, COLS)
+    mix_s[pl.ds(4 * h, 4)] = mix_s[pl.ds(4 * h, 4)] + added[:, 0:TOK]
+    mix = []
+    for i, other in enumerate(near + far):
+        mix_r[8 + i] = mix_s[other].astype(BF)
+        copy = remote(mix_r.at[8 + i], mix_r.at[i], mx_s.at[i], mx_r.at[i], (other * X + x, dp))
+        copy.start()
+        mix.append(copy)
+    ring_step(0, 5)
+    ring_step(2, 4)
+    for copy in back[14:]:
+        copy.wait()
+    mix_c[...] = dot(gt_c[...], back_c[...].reshape(HALF, COLS)).reshape(4, LANES, COLS)[:, 0:TOK]
+    for i, other in enumerate(near):
+        mixc_r[4 + i] = mix_c[other % 4].astype(BF)
+        copy = remote(mixc_r.at[4 + i], mixc_r.at[i], mxc_s.at[i], mxc_r.at[i], (other * X + x, dp))
+        copy.start()
+        mix.append(copy)
+    ring_step(0, 6)
     ring_step(2, 5)
     ring_step(2, 6)
 
@@ -454,11 +466,13 @@
         hg_ref[1, :, at] = (value_n[side] * cold + val_h[:, at] * hot).astype(BF)
     hg_ref[2] = val_c[...].astype(BF)
 
-    total = mix_s[z]
+    total = mix_s[z] + mix_c[z % 4]
     for copy in mix:
         copy.wait()
     for i in range(Z - 1):
         total = total + mix_r[i].astype(F32)
+    for i in range(3):
+        total = total + mixc_r[i].astype(F32)
     mixed_ref[...] = total.astype(BF)
 
     for kind in range(3):
@@ -496,20 +510,20 @@
         b(2, COLS, H), b(COLS, H), b(COLS, H), b(COLS, H),
         b(Z, 2 * TOP, LANES), b(Z, LANES, COLS), b(2 * HALF, 2 * HALF), b(HALF, HALF),
         f(X, Z * LANES), f(X, 4 * LANES), f(X, 4 * LANES), f(X, Z * LANES), f(X, 4 * LANES), f(X, 4 * LANES),
-        b(X * TOK, Z * LANES), b(X * TOK, 4 * LANES), b(Z * LANES, X * TOK), b(4 * LANES, X * TOK),
+        b(X * TOK, Z * LANES), b(X * TOK, 4 * LANES), b(Z * LANES, X * TOK), b(4 * LANES, HALF), b(4 * LANES, HALF),
         b(2 * HALF, COLS), b(HALF, COLS), b(HALF, COLS),
         b(X, TOK, COLS), b(X, TOK, COLS), b(X, TOK, COLS), b(X, TOK, COLS),
-        b(X, TOK, COLS), b(X, BLOCK, COLS), b(X, BLOCK, COLS), b(X, TOK, COLS), b(X, TOK, COLS),
+        b(X, TOK, COLS), b(X, BLOCK, COLS), b(X, BLOCK, COLS), b(X, TOK, COLS), b(X, BLOCK, COLS), b(X, BLOCK, COLS),
         b(2 * HALF, COLS), b(2 * HALF, COLS), b(COLS, 2 * HALF), b(COLS, 2 * HALF),
         b(2, 8, BLOCK, SIDE), b(2, 4, BLOCK, SIDE), b(2, 4, BLOCK, SIDE),
         b(2, 8, BLOCK, SIDE), b(2, 4, BLOCK, SIDE), b(2, 4, BLOCK, SIDE),
         f(2, 8, BLOCK, SIDE), f(2, 4, BLOCK, SIDE), f(2, 4, BLOCK, SIDE),
         b(2, RING, BLOCK, SIDE), b(2, RING, BLOCK, SIDE), b(2, RING, BLOCK, SIDE),
         b(2, RING, BLOCK, SIDE), b(2, RING, BLOCK, SIDE), b(2, RING, BLOCK, SIDE),
-        f(Z, TOK, COLS), b(2 * Z, TOK, COLS), f(BLOCK, H), f(BLOCK, H), b(2, COLS, H), b(1, COLS, H),
+        f(Z, TOK, COLS), b(2 * Z, TOK, COLS), f(4, TOK, COLS), b(8, TOK, COLS), f(BLOCK, H), f(BLOCK, H), b(2, COLS, H), b(1, COLS, H),
         dma((4,)), dma((7,)), dma((7,)), dma((7,)), dma((7,)), dma((1,)), dma((1,)),
         dma((7,)), dma((7,)), dma((7,)), dma((7,)), dma((7,)), dma((7,)), dma((7,)), dma((7,)), dma((7,)), dma((7,)),
-        dma((6,)), dma((6,)), dma((6 * RING,)), dma((6 * RING,)), dma((7,)), dma((7,)), dma((2,)),
+        dma((6,)), dma((6,)), dma((6 * RING,)), dma((6 * RING,)), dma((7,)), dma((7,)), dma((3,)), dma((3,)), dma((2,)),
     ]
     shapes = (
         jax.ShapeDtypeStruct((TOK, COLS), BF),

time: 95.2 us -> 99.1 us (1.041)
  the two profiles are of different devices: /device:TPU:16 before, /device:TPU:128 now
where the time goes in v4:
time: 99.1 us; the launch traced here: 98.9 us
  Pallas kernels  98.3 us (99%)
    pallas_call x1, Pallas kernels, body(): pl.pallas_call(kernel, out_shape=shapes, in_specs=[anywhere, anywhere, vm...  95.8 us
    pallas_call x1, Pallas kernels, body(): pl.pallas_call(store, out_shape=shapes, in_specs=[anywhere] * 4, out_spec...  2.44 us

profile of v4, /device:TPU:128, one launch (start us, length us, event | category | flops | bytes accessed | tf_op | source)
XLA Modules:
  0.0 98.9 jit_solution(18399915714067385444)
XLA Ops:
  0.6 95.8 %experts.1 = (bf16[96,224]{1,0:T(8,128)(2,1)}, bf16[3,48,1024]{2,1,0:T(8,128)(2,1)}, bf16[2,224,1024]{2,1,0:T(8,128)(2,1)}, bf16[1,224,1024]{2,1,0:T(8,128)(2,1)}) custom-call(bf16[3,768,1024]{2,1,0:T(8,128)(2,1)} %hid_hbm.1, bf16[2,224,1024]{2,1,0:T(8,128)(2,1)} %bitcast.6, bf16[96,224]{1,0:T(8,128)(2,1)} %og_ref.1, s32[8,96]{1,0:T(8,128)} %bitcast.7, ...), custom_call_target="tpu_custom_call" | custom-call | tf_op jit(solution)/shard_map/experts/pallas_call | solution.py:534
  96.5 2.4 %store.1 = (bf16[96,224]{1,0:T(8,128)(2,1)}, bf16[3,48,1024]{2,1,0:T(8,128)(2,1)}, bf16[2,224,1024]{2,1,0:T(8,128)(2,1)}, bf16[1,224,1024]{2,1,0:T(8,128)(2,1)}) custom-call(bf16[96,224]{1,0:T(8,128)(2,1)} %get-tuple-element.12.refs_0_, bf16[3,48,1024]{2,1,0:T(8,128)(2,1)} %get-tuple-element.13.refs_1_, bf16[2,224,1024]{2,1,0:T(8,128)(2,1)} %get-tuple-element.14.refs_2_, ...), custom_call_target="tpu_custom_call" | custom-call | tf_op jit(solution)/shard_map/store/pallas_call | solution.py:552

commit v5 on v4

--- a/solution.py
+++ b/solution.py
@@ -40,15 +40,15 @@
     hid_hbm, w_hbm, og_ref, ids_ref, code_ref, load_ref,
     mixed_ref, hg_ref, wg_hbm, sg_hbm,
     hid, hid_n, hid_h, hid_c, w, w_n, w_h, w_c,
-    meta, tok, perm, perm_h,
+    meta, tok, perm, perm_h, perm_r,
     key_n, key_h, key_c, gate_n, gate_h, gate_c, g_n, g_hc, gt_n, gt_h, gt_c,
-    out_n, out_h, out_c, send_n, send_hc, recv_n, recv_hc,
+    out_n, out_h, out_c, send_n, send_hc, recv_n, recv_h, recv_c,
     sb_n, sb_h, sb_c, back_n, back_h, back_c, rg_n, rg_hc, rgt_n, rgt_hc,
     cxs_n, cxs_h, cxs_c, cxr_n, cxr_h, cxr_c, sum_n, sum_h, sum_c,
     rs_n, rs_h, rs_c, rr_n, rr_h, rr_c,
-    mix_s, mix_r, mix_c, mixc_r, val_h, val_c, wg, sg,
+    mix_s, mix_r, mix_c, mixc_r, val_h, val_c, grad_h, wg, sg,
     load_sem, zt_s, zt_r, zm_s, zm_r, wc_s, wc_r,
-    dn_s, dn_r, dh_s, dh_r, bn_s, bn_r, bh_s, bh_r, bc_s, bc_r,
+    dn_s, dn_r, dh_s, dh_r, dc_s, dc_r, bn_s, bn_r, bh_s, bh_r, bc_s, bc_r,
     cx_s, cx_r, ring_s, ring_r, mx_s, mx_r, mxc_s, mxc_r, out_sem,
 ):
     e = lax.axis_index("expert")
@@ -139,6 +139,7 @@
         perm[k * TOK : (k + 1) * TOK] = jnp.where(col == moved + k * MOST, 1.0, 0.0).astype(BF)
     for k in range(8):
         perm_h[k * BLOCK : (k + 1) * BLOCK] = perm[k * TOK : k * TOK + BLOCK, 0:HALF]
+    perm_r[...] = perm_h[...].astype(F32).T.astype(BF)
 
     loads[1].wait()
     loads[2].wait()
@@ -214,11 +215,14 @@
         for d in group:
             i = order.index(d)
             if d:
-                copy = remote(send_hc.at[i], recv_hc.at[x], dh_s.at[i - 1], dh_r.at[i - 1], x_peer(d))
+                copy = remote(
+                    send_hc.at[i, pl.ds(0, BLOCK)], recv_h.at[x], dh_s.at[i - 1], dh_r.at[i - 1], x_peer(d)
+                )
                 copy.start()
                 dispatch_h.append(copy)
             else:
-                recv_hc[x] = send_hc[i]
+                recv_h[x] = send_hc[i, 0:BLOCK]
+                recv_c[x] = send_hc[i, BLOCK:TOK]
 
     for copy in gather[6:]:
         copy.wait()
@@ -245,6 +249,15 @@
             else:
                 recv_n[x] = send_n[i]
 
+    dispatch_c = []
+    for i, d in enumerate(order):
+        if d:
+            copy = remote(
+                send_hc.at[i, pl.ds(BLOCK, BLOCK)], recv_c.at[x], dc_s.at[i - 1], dc_r.at[i - 1], x_peer(d)
+            )
+            copy.start()
+            dispatch_c.append(copy)
+
     def forward_h(i, carry):
         at = pl.ds(pl.multiple_of(i * 128, 128), 128)
         far = pl.ds(pl.multiple_of(h * HALF + i * 128, 128), 128)
@@ -334,9 +347,7 @@
 
     for copy in dispatch_h:
         copy.wait()
-    for i in range(2):
-        rows = dot(perm[i * HALF : (i + 1) * HALF], recv_hc[...].reshape(2 * HALF, COLS)).astype(BF)
-        rg_hc[i * HALF : (i + 1) * HALF] = rows
+    rg_hc[0:HALF] = dot(perm_r[...], recv_h[...].reshape(HALF, COLS)).astype(BF)
     pair_h = partial(rg_hc, 0, 4, w_h, cxs_h, cxr_h, sum_h, 2)
     for i, d in enumerate((4, 3, -3, 2, -2, 1, -1)):
         copy = remote(
@@ -345,10 +356,22 @@
         copy.start()
         back.append(copy)
     back_h[0] = sb_h[x]
+
+    scale = 2.0 / TOK
+    rgt_hc[:, 0:HALF] = rg_hc[0:HALF].T
+    for i in range(2):
+        at = slice(i * SIDE, (i + 1) * SIDE)
+        grad_h[:, at] = scale * dot(rgt_hc[:, 0:HALF], hid_h[:, at])
     for copy in pair_h:
         copy.wait()
     ring_step(1, 0)
+
+    for copy in back[0:7]:
+        copy.wait()
+    rows = jnp.concatenate([back_n[d] for d in order], axis=0)
+    mix_s[...] = dot(gt_n[...], rows).reshape(Z, LANES, COLS)[:, 0:TOK]
     ring_step(1, 1)
+
     for copy in dispatch_n:
         copy.wait()
     for i in range(2):
@@ -356,9 +379,28 @@
         rg_n[i * HALF : (i + 1) * HALF] = rows
     pair_n = partial(rg_n, 0, 8, w_n, cxs_n, cxr_n, sum_n, 0)
     ring_step(1, 2)
+
     for copy in pair_n:
         copy.wait()
     ring_step(0, 0)
+    rgt_n[...] = rg_n[...].T
+    ring_step(1, 3)
+    ring_step(0, 1)
+
+    def weight_part(i):
+        at = slice(i * 256, (i + 1) * 256)
+        grad_n = scale * dot(rgt_n[...], hid_n[:, at])
+        wg[0, :, at] = (grad_n * hot + grad_h[:, at] * cold).astype(BF)
+        wg[1, :, at] = (grad_n * cold + grad_h[:, at] * hot).astype(BF)
+
+    def spare_part(i):
+        at = slice(i * SIDE, (i + 1) * SIDE)
+        sg[0, :, at] = (scale * dot(rgt_hc[:, HALF : 2 * HALF], hid_c[:, at])).astype(BF)
+
+    weight_part(0)
+    weight_part(1)
+    ring_step(1, 4)
+    ring_step(0, 2)
 
     spare.wait()
     loads[3].wait()
@@ -378,50 +420,21 @@
         copy.start()
         back.append(copy)
     back_c[0] = sb_c[x]
+    for copy in dispatch_c:
+        copy.wait()
+    rg_hc[HALF : 2 * HALF] = dot(perm_r[...], recv_c[...].reshape(HALF, COLS)).astype(BF)
     pair_c = partial(rg_hc, HALF, 4, w_c, cxs_c, cxr_c, sum_c, 4)
-    ring_step(1, 3)
-    ring_step(0, 1)
-    for copy in pair_c:
-        copy.wait()
-    ring_step(2, 0)
-
-    scale = 2.0 / TOK
-
-    def turn_rows():
-        rgt_n[...] = rg_n[...].T
-        rgt_hc[...] = rg_hc[...].T
-
-    def weight_part(i):
-        at = slice(i * SIDE, (i + 1) * SIDE)
-        grad_n = scale * dot(rgt_n[...], hid_n[:, at])
-        grad_h = scale * dot(rgt_hc[:, 0:HALF], hid_h[:, at])
-        wg[0, :, at] = (grad_n * hot + grad_h * cold).astype(BF)
-        wg[1, :, at] = (grad_n * cold + grad_h * hot).astype(BF)
-        sg[0, :, at] = (scale * dot(rgt_hc[:, HALF : 2 * HALF], hid_c[:, at])).astype(BF)
-
-    turn_rows()
-    ring_step(1, 4)
-    ring_step(0, 2)
-    ring_step(2, 1)
-    weight_part(0)
     ring_step(1, 5)
     ring_step(0, 3)
-    ring_step(2, 2)
-    weight_part(1)
-    stores = [
-        pltpu.make_async_copy(wg, wg_hbm, out_sem.at[0]),
-        pltpu.make_async_copy(sg, sg_hbm, out_sem.at[1]),
-    ]
-    for copy in stores:
-        copy.start()
+    rgt_hc[:, HALF : 2 * HALF] = rg_hc[HALF : 2 * HALF].T
+    for copy in pair_c:
+        copy.wait()
+    ring_step(2, 0)
     ring_step(1, 6)
     ring_step(0, 4)
-    ring_step(2, 3)
-
-    for copy in back[0:14]:
-        copy.wait()
-    rows = jnp.concatenate([back_n[d] for d in order], axis=0)
-    mix_s[...] = dot(gt_n[...], rows).reshape(Z, LANES, COLS)[:, 0:TOK]
+
+    for copy in back[7:14]:
+        copy.wait()
     added = dot(gt_h[...], back_h[...].reshape(HALF, COLS)).reshape(4, LANES, COLS)
     mix_s[pl.ds(4 * h, 4)] = mix_s[pl.ds(4 * h, 4)] + added[:, 0:TOK]
     mix = []
@@ -430,8 +443,13 @@
         copy = remote(mix_r.at[8 + i], mix_r.at[i], mx_s.at[i], mx_r.at[i], (other * X + x, dp))
         copy.start()
         mix.append(copy)
+    ring_step(2, 1)
     ring_step(0, 5)
-    ring_step(2, 4)
+    weight_part(2)
+    ring_step(2, 2)
+    ring_step(0, 6)
+    weight_part(3)
+    ring_step(2, 3)
     for copy in back[14:]:
         copy.wait()
     mix_c[...] = dot(gt_c[...], back_c[...].reshape(HALF, COLS)).reshape(4, LANES, COLS)[:, 0:TOK]
@@ -440,8 +458,16 @@
         copy = remote(mixc_r.at[4 + i], mixc_r.at[i], mxc_s.at[i], mxc_r.at[i], (other * X + x, dp))
         copy.start()
         mix.append(copy)
-    ring_step(0, 6)
+    ring_step(2, 4)
+    spare_part(0)
     ring_step(2, 5)
+    spare_part(1)
+    stores = [
+        pltpu.make_async_copy(wg, wg_hbm, out_sem.at[0]),
+        pltpu.make_async_copy(sg, sg_hbm, out_sem.at[1]),
+    ]
+    for copy in stores:
+        copy.start()
     ring_step(2, 6)
 
     val_h[...] = jnp.zeros_like(val_h)
@@ -508,11 +534,11 @@
     scratch = [
         b(2, 2 * HALF, H), b(2 * HALF, H), b(HALF, H), b(HALF, H),
         b(2, COLS, H), b(COLS, H), b(COLS, H), b(COLS, H),
-        b(Z, 2 * TOP, LANES), b(Z, LANES, COLS), b(2 * HALF, 2 * HALF), b(HALF, HALF),
+        b(Z, 2 * TOP, LANES), b(Z, LANES, COLS), b(2 * HALF, 2 * HALF), b(HALF, HALF), b(HALF, HALF),
         f(X, Z * LANES), f(X, 4 * LANES), f(X, 4 * LANES), f(X, Z * LANES), f(X, 4 * LANES), f(X, 4 * LANES),
         b(X * TOK, Z * LANES), b(X * TOK, 4 * LANES), b(Z * LANES, X * TOK), b(4 * LANES, HALF), b(4 * LANES, HALF),
         b(2 * HALF, COLS), b(HALF, COLS), b(HALF, COLS),
-        b(X, TOK, COLS), b(X, TOK, COLS), b(X, TOK, COLS), b(X, TOK, COLS),
+        b(X, TOK, COLS), b(X, TOK, COLS), b(X, TOK, COLS), b(X, BLOCK, COLS), b(X, BLOCK, COLS),
         b(X, TOK, COLS), b(X, BLOCK, COLS), b(X, BLOCK, COLS), b(X, TOK, COLS), b(X, BLOCK, COLS), b(X, BLOCK, COLS),
         b(2 * HALF, COLS), b(2 * HALF, COLS), b(COLS, 2 * HALF), b(COLS, 2 * HALF),
         b(2, 8, BLOCK, SIDE), b(2, 4, BLOCK, SIDE), b(2, 4, BLOCK, SIDE),
@@ -520,9 +546,9 @@
         f(2, 8, BLOCK, SIDE), f(2, 4, BLOCK, SIDE), f(2, 4, BLOCK, SIDE),
         b(2, RING, BLOCK, SIDE), b(2, RING, BLOCK, SIDE), b(2, RING, BLOCK, SIDE),
         b(2, RING, BLOCK, SIDE), b(2, RING, BLOCK, SIDE), b(2, RING, BLOCK, SIDE),
-        f(Z, TOK, COLS), b(2 * Z, TOK, COLS), f(4, TOK, COLS), b(8, TOK, COLS), f(BLOCK, H), f(BLOCK, H), b(2, COLS, H), b(1, COLS, H),
+        f(Z, TOK, COLS), b(2 * Z, TOK, COLS), f(4, TOK, COLS), b(8, TOK, COLS), f(BLOCK, H), f(BLOCK, H), f(COLS, H), b(2, COLS, H), b(1, COLS, H),
         dma((4,)), dma((7,)), dma((7,)), dma((7,)), dma((7,)), dma((1,)), dma((1,)),
-        dma((7,)), dma((7,)), dma((7,)), dma((7,)), dma((7,)), dma((7,)), dma((7,)), dma((7,)), dma((7,)), dma((7,)),
+        dma((7,)), dma((7,)), dma((7,)), dma((7,)), dma((7,)), dma((7,)), dma((7,)), dma((7,)), dma((7,)), dma((7,)), dma((7,)), dma((7,)),
         dma((6,)), dma((6,)), dma((6 * RING,)), dma((6 * RING,)), dma((7,)), dma((7,)), dma((3,)), dma((3,)), dma((2,)),
     ]
     shapes = (

time: 99.1 us -> 108 us (1.090)
  the two profiles are of different devices: /device:TPU:128 before, /device:TPU:270 now
where the time goes in v5:
time: 108 us
  Pallas kernels  107 us (99%)
    pallas_call x1, Pallas kernels, body(): pl.pallas_call(kernel, out_shape=shapes, in_specs=[anywhere, anywhere, vm...  105 us
    pallas_call x1, Pallas kernels, body(): pl.pallas_call(store, out_shape=shapes, in_specs=[anywhere] * 4, out_spec...  2.44 us

profile of v5, /device:TPU:270, one launch (start us, length us, event | category | flops | bytes accessed | tf_op | source)
XLA Modules:
  0.0 107.8 jit_solution(6198061003312863105)
XLA Ops:
  0.6 104.8 %experts.1 = (bf16[96,224]{1,0:T(8,128)(2,1)}, bf16[3,48,1024]{2,1,0:T(8,128)(2,1)}, bf16[2,224,1024]{2,1,0:T(8,128)(2,1)}, bf16[1,224,1024]{2,1,0:T(8,128)(2,1)}) custom-call(bf16[3,768,1024]{2,1,0:T(8,128)(2,1)} %hid_hbm.1, bf16[2,224,1024]{2,1,0:T(8,128)(2,1)} %bitcast.6, bf16[96,224]{1,0:T(8,128)(2,1)} %og_ref.1, s32[8,96]{1,0:T(8,128)} %bitcast.7, ...), custom_call_target="tpu_custom_call" | custom-call | tf_op jit(solution)/shard_map/experts/pallas_call | solution.py:560
  105.4 2.4 %store.1 = (bf16[96,224]{1,0:T(8,128)(2,1)}, bf16[3,48,1024]{2,1,0:T(8,128)(2,1)}, bf16[2,224,1024]{2,1,0:T(8,128)(2,1)}, bf16[1,224,1024]{2,1,0:T(8,128)(2,1)}) custom-call(bf16[96,224]{1,0:T(8,128)(2,1)} %get-tuple-element.12.refs_0_, bf16[3,48,1024]{2,1,0:T(8,128)(2,1)} %get-tuple-element.13.refs_1_, bf16[2,224,1024]{2,1,0:T(8,128)(2,1)} %get-tuple-element.14.refs_2_, ...), custom_call_target="tpu_custom_call" | custom-call | tf_op jit(solution)/shard_map/store/pallas_call | solution.py:578

commit v6 on v4

--- a/solution.py
+++ b/solution.py
@@ -46,7 +46,7 @@
     sb_n, sb_h, sb_c, back_n, back_h, back_c, rg_n, rg_hc, rgt_n, rgt_hc,
     cxs_n, cxs_h, cxs_c, cxr_n, cxr_h, cxr_c, sum_n, sum_h, sum_c,
     rs_n, rs_h, rs_c, rr_n, rr_h, rr_c,
-    mix_s, mix_r, mix_c, mixc_r, val_h, val_c, wg, sg,
+    mix_s, mix_r, mix_c, mixc_r, val_h, val_c, grad_h, wg, sg,
     load_sem, zt_s, zt_r, zm_s, zm_r, wc_s, wc_r,
     dn_s, dn_r, dh_s, dh_r, bn_s, bn_r, bh_s, bh_r, bc_s, bc_r,
     cx_s, cx_r, ring_s, ring_r, mx_s, mx_r, mxc_s, mxc_r, out_sem,
@@ -345,10 +345,24 @@
         copy.start()
         back.append(copy)
     back_h[0] = sb_h[x]
+
+    scale = 2.0 / TOK
+    loads[3].wait()
+    rgt_hc[...] = rg_hc[...].T
+    for i in range(2):
+        at = slice(i * SIDE, (i + 1) * SIDE)
+        grad_h[:, at] = scale * dot(rgt_hc[:, 0:HALF], hid_h[:, at])
+        sg[0, :, at] = (scale * dot(rgt_hc[:, HALF : 2 * HALF], hid_c[:, at])).astype(BF)
     for copy in pair_h:
         copy.wait()
     ring_step(1, 0)
+
+    for copy in back[0:7]:
+        copy.wait()
+    rows = jnp.concatenate([back_n[d] for d in order], axis=0)
+    mix_s[...] = dot(gt_n[...], rows).reshape(Z, LANES, COLS)[:, 0:TOK]
     ring_step(1, 1)
+
     for copy in dispatch_n:
         copy.wait()
     for i in range(2):
@@ -356,12 +370,8 @@
         rg_n[i * HALF : (i + 1) * HALF] = rows
     pair_n = partial(rg_n, 0, 8, w_n, cxs_n, cxr_n, sum_n, 0)
     ring_step(1, 2)
-    for copy in pair_n:
-        copy.wait()
-    ring_step(0, 0)
 
     spare.wait()
-    loads[3].wait()
 
     def forward_c(i, carry):
         at = pl.ds(pl.multiple_of(i * 128, 128), 128)
@@ -378,6 +388,9 @@
         copy.start()
         back.append(copy)
     back_c[0] = sb_c[x]
+    for copy in pair_n:
+        copy.wait()
+    ring_step(0, 0)
     pair_c = partial(rg_hc, HALF, 4, w_c, cxs_c, cxr_c, sum_c, 4)
     ring_step(1, 3)
     ring_step(0, 1)
@@ -385,43 +398,19 @@
         copy.wait()
     ring_step(2, 0)
 
-    scale = 2.0 / TOK
-
-    def turn_rows():
-        rgt_n[...] = rg_n[...].T
-        rgt_hc[...] = rg_hc[...].T
-
     def weight_part(i):
-        at = slice(i * SIDE, (i + 1) * SIDE)
+        at = slice(i * 256, (i + 1) * 256)
         grad_n = scale * dot(rgt_n[...], hid_n[:, at])
-        grad_h = scale * dot(rgt_hc[:, 0:HALF], hid_h[:, at])
-        wg[0, :, at] = (grad_n * hot + grad_h * cold).astype(BF)
-        wg[1, :, at] = (grad_n * cold + grad_h * hot).astype(BF)
-        sg[0, :, at] = (scale * dot(rgt_hc[:, HALF : 2 * HALF], hid_c[:, at])).astype(BF)
-
-    turn_rows()
+        wg[0, :, at] = (grad_n * hot + grad_h[:, at] * cold).astype(BF)
+        wg[1, :, at] = (grad_n * cold + grad_h[:, at] * hot).astype(BF)
+
+    rgt_n[...] = rg_n[...].T
     ring_step(1, 4)
     ring_step(0, 2)
     ring_step(2, 1)
-    weight_part(0)
-    ring_step(1, 5)
-    ring_step(0, 3)
-    ring_step(2, 2)
-    weight_part(1)
-    stores = [
-        pltpu.make_async_copy(wg, wg_hbm, out_sem.at[0]),
-        pltpu.make_async_copy(sg, sg_hbm, out_sem.at[1]),
-    ]
-    for copy in stores:
-        copy.start()
-    ring_step(1, 6)
-    ring_step(0, 4)
-    ring_step(2, 3)
-
-    for copy in back[0:14]:
-        copy.wait()
-    rows = jnp.concatenate([back_n[d] for d in order], axis=0)
-    mix_s[...] = dot(gt_n[...], rows).reshape(Z, LANES, COLS)[:, 0:TOK]
+
+    for copy in back[7:14]:
+        copy.wait()
     added = dot(gt_h[...], back_h[...].reshape(HALF, COLS)).reshape(4, LANES, COLS)
     mix_s[pl.ds(4 * h, 4)] = mix_s[pl.ds(4 * h, 4)] + added[:, 0:TOK]
     mix = []
@@ -430,8 +419,13 @@
         copy = remote(mix_r.at[8 + i], mix_r.at[i], mx_s.at[i], mx_r.at[i], (other * X + x, dp))
         copy.start()
         mix.append(copy)
-    ring_step(0, 5)
-    ring_step(2, 4)
+    ring_step(1, 5)
+    ring_step(0, 3)
+    ring_step(2, 2)
+    weight_part(0)
+    ring_step(1, 6)
+    ring_step(0, 4)
+    ring_step(2, 3)
     for copy in back[14:]:
         copy.wait()
     mix_c[...] = dot(gt_c[...], back_c[...].reshape(HALF, COLS)).reshape(4, LANES, COLS)[:, 0:TOK]
@@ -440,9 +434,20 @@
         copy = remote(mixc_r.at[4 + i], mixc_r.at[i], mxc_s.at[i], mxc_r.at[i], (other * X + x, dp))
         copy.start()
         mix.append(copy)
+    ring_step(0, 5)
+    ring_step(2, 4)
+    weight_part(1)
     ring_step(0, 6)
     ring_step(2, 5)
+    weight_part(2)
     ring_step(2, 6)
+    weight_part(3)
+    stores = [
+        pltpu.make_async_copy(wg, wg_hbm, out_sem.at[0]),
+        pltpu.make_async_copy(sg, sg_hbm, out_sem.at[1]),
+    ]
+    for copy in stores:
+        copy.start()
 
     val_h[...] = jnp.zeros_like(val_h)
     val_c[...] = jnp.zeros_like(val_c)
@@ -520,7 +525,7 @@
         f(2, 8, BLOCK, SIDE), f(2, 4, BLOCK, SIDE), f(2, 4, BLOCK, SIDE),
         b(2, RING, BLOCK, SIDE), b(2, RING, BLOCK, SIDE), b(2, RING, BLOCK, SIDE),
         b(2, RING, BLOCK, SIDE), b(2, RING, BLOCK, SIDE), b(2, RING, BLOCK, SIDE),
-        f(Z, TOK, COLS), b(2 * Z, TOK, COLS), f(4, TOK, COLS), b(8, TOK, COLS), f(BLOCK, H), f(BLOCK, H), b(2, COLS, H), b(1, COLS, H),
+        f(Z, TOK, COLS), b(2 * Z, TOK, COLS), f(4, TOK, COLS), b(8, TOK, COLS), f(BLOCK, H), f(BLOCK, H), f(COLS, H), b(2, COLS, H), b(1, COLS, H),
         dma((4,)), dma((7,)), dma((7,)), dma((7,)), dma((7,)), dma((1,)), dma((1,)),
         dma((7,)), dma((7,)), dma((7,)), dma((7,)), dma((7,)), dma((7,)), dma((7,)), dma((7,)), dma((7,)), dma((7,)),
         dma((6,)), dma((6,)), dma((6 * RING,)), dma((6 * RING,)), dma((7,)), dma((7,)), dma((3,)), dma((3,)), dma((2,)),

time: 99.1 us -> 99.5 us (level)
  no operation moved by 1% of the time
where the time goes in v6:
time: 99.5 us; the launch traced here: 99.3 us
  Pallas kernels  98.7 us (99%)
    pallas_call x1, Pallas kernels, body(): pl.pallas_call(kernel, out_shape=shapes, in_specs=[anywhere, anywhere, vm...  96.2 us
    pallas_call x1, Pallas kernels, body(): pl.pallas_call(store, out_shape=shapes, in_specs=[anywhere] * 4, out_spec...  2.44 us

profile of v6, /device:TPU:128, one launch (start us, length us, event | category | flops | bytes accessed | tf_op | source)
XLA Modules:
  0.0 99.3 jit_solution(1588689230187668148)
XLA Ops:
  0.6 96.2 %experts.1 = (bf16[96,224]{1,0:T(8,128)(2,1)}, bf16[3,48,1024]{2,1,0:T(8,128)(2,1)}, bf16[2,224,1024]{2,1,0:T(8,128)(2,1)}, bf16[1,224,1024]{2,1,0:T(8,128)(2,1)}) custom-call(bf16[3,768,1024]{2,1,0:T(8,128)(2,1)} %hid_hbm.1, bf16[2,224,1024]{2,1,0:T(8,128)(2,1)} %bitcast.6, bf16[96,224]{1,0:T(8,128)(2,1)} %og_ref.1, s32[8,96]{1,0:T(8,128)} %bitcast.7, ...), custom_call_target="tpu_custom_call" | custom-call | tf_op jit(solution)/shard_map/experts/pallas_call | solution.py:539
  96.9 2.4 %store.1 = (bf16[96,224]{1,0:T(8,128)(2,1)}, bf16[3,48,1024]{2,1,0:T(8,128)(2,1)}, bf16[2,224,1024]{2,1,0:T(8,128)(2,1)}, bf16[1,224,1024]{2,1,0:T(8,128)(2,1)}) custom-call(bf16[96,224]{1,0:T(8,128)(2,1)} %get-tuple-element.12.refs_0_, bf16[3,48,1024]{2,1,0:T(8,128)(2,1)} %get-tuple-element.13.refs_1_, bf16[2,224,1024]{2,1,0:T(8,128)(2,1)} %get-tuple-element.14.refs_2_, ...), custom_call_target="tpu_custom_call" | custom-call | tf_op jit(solution)/shard_map/store/pallas_call | solution.py:557
